TPU v7x, 256 devices: a whole 4x4x8 slice. The times are simulated.
256 devices in a mesh: resp: 64 (over x, y_lo, z), kvh: 4 (over y_hi, core).
Axes of the slice: x: 4, y: 4 (y_hi: 2, y_lo: 2; y = y_hi * 2 + y_lo), z: 8, core: 2. Of those that a mesh axis runs over, the one named last changes fastest.
Arguments:
- query: bfloat16 [16384, 5120], P('resp', 'kvh'), may hold values from -5 to 5
- response_keys: bfloat16 [16384, 1024], P('resp', 'kvh'), may hold values from -5 to 5
- response_values: bfloat16 [16384, 1024], P('resp', 'kvh'), may hold values from -5 to 5
- prompt_key: bfloat16 [2048, 1024], P(('resp', 'kvh')), may hold values from -5 to 5
- prompt_values: bfloat16 [2048, 1024], P(('resp', 'kvh')), may hold values from -5 to 5
- out_grad: bfloat16 [16384, 5120], P('resp', 'kvh'), may hold values from -5 to 5
- lengths: int32 [64, 2], P('resp'), may hold values from 1 to 192, 256 in all within a row
- advantage: float32 [64, 2], P('resp'), may hold values from -3 to 3
Outputs:
- grad_query: bfloat16 [16384, 5120], P('resp', 'kvh')
- grad_resp_key: bfloat16 [16384, 1024], P('resp', 'kvh')
- grad_resp_value: bfloat16 [16384, 1024], P('resp', 'kvh')
- grad_prompt_key: float32 [2048, 1024], P(('resp', 'kvh'))
- grad_prompt_value: float32 [2048, 1024], P(('resp', 'kvh'))
Inputs may be any that keep to these rules, and one draw needn't show every extreme that they name: Each row of lengths sums to 256; its split into two lengths is drawn at random.
All inputs are finite; a program needn't handle non-finite values.
Results may differ from a plain program's by a relative error of at most 0.012.
Values may be sent and summed in bfloat16 or wider, within the bound.
No kernel may reach another device: no remote copies, remote signals or barrier semaphores. Data moves between devices by JAX's collectives and lax.ppermute only.
A program may use at most 128 MiB of HBM per device.

v0:
```python
import math

import jax
import jax.numpy as jnp
from jax import lax
from jax.sharding import PartitionSpec as P

QUERY_HEADS = 40
KEY_VALUE_HEADS = 8
HEAD_SIZE = 128


def head_scores(query_block, key_row_block, factor):
    return (
        jnp.einsum("bhgd,khd->hgbk", query_block, key_row_block, preferred_element_type=jnp.float32)
        * factor
    )


def block_backward(
    query_block, gradient_rows, key_row_block, value_row_block, softmax, row_delta, factor
):
    rounded_length = softmax.astype(jnp.bfloat16)
    prob_grad = jnp.einsum(
        "bhgd,khd->hgbk", gradient_rows, value_row_block, preferred_element_type=jnp.float32
    )
    score_gradient = (softmax * (prob_grad - row_delta[..., None]) * factor).astype(jnp.bfloat16)
    query_part = jnp.einsum(
        "hgbk,khd->bhgd", score_gradient, key_row_block, preferred_element_type=jnp.float32
    )
    key_part = jnp.einsum(
        "rlev,erlp->vrp", score_gradient, query_block, preferred_element_type=jnp.float32
    )
    value_part = jnp.einsum(
        "rlev,erlp->vrp", rounded_length, gradient_rows, preferred_element_type=jnp.float32
    )
    return (query_part, key_part, value_part)


def on_device(
    query, response_keys, response_values, prompt_key, prompt_values, out_grad, lengths, advantage
):
    tok_rows = query.shape[0]
    heads_here = response_keys.shape[1] // HEAD_SIZE
    own_cols = heads_here * HEAD_SIZE
    query_group = QUERY_HEADS // KEY_VALUE_HEADS
    factor = 1.0 / math.sqrt(HEAD_SIZE)
    positions = jnp.arange(tok_rows, dtype=jnp.int32)
    resp_ends = jnp.cumsum(lengths[0])
    segment = jnp.sum((positions[:, None] >= resp_ends[None, :]).astype(jnp.int32), axis=1)
    labels = jnp.arange(lengths.shape[1], dtype=jnp.int32)
    weight = jnp.sum(
        jnp.where(segment[:, None] == labels[None, :], advantage[0][None, :], 0.0), axis=1
    )
    grad_out = (weight[:, None] * out_grad.astype(jnp.float32)).astype(jnp.bfloat16)
    query_block = query.reshape(tok_rows, heads_here, query_group, HEAD_SIZE)
    gradient_rows = grad_out.reshape(tok_rows, heads_here, query_group, HEAD_SIZE)
    near_key = response_keys.reshape(tok_rows, heads_here, HEAD_SIZE)
    near_value = response_values.reshape(tok_rows, heads_here, HEAD_SIZE)
    allowed = (segment[None, :] == segment[:, None]) & (positions[None, :] <= positions[:, None])
    head_key, head_value = (
        lax.all_to_all(prompt_key, "kvh", split_axis=1, concat_axis=0, tiled=True),
        lax.all_to_all(prompt_values, "kvh", split_axis=1, concat_axis=0, tiled=True),
    )
    all_key, all_value = (
        lax.all_gather(head_key, "resp", axis=0, tiled=True),
        lax.all_gather(head_value, "resp", axis=0, tiled=True),
    )
    prompt_len = all_key.shape[0]
    full_key = all_key.reshape(prompt_len, heads_here, HEAD_SIZE)
    full_value = all_value.reshape(prompt_len, heads_here, HEAD_SIZE)
    block_rows = math.gcd(prompt_len, 512)
    block_count = prompt_len // block_rows
    near_scores = jnp.where(allowed[None, None], head_scores(query_block, near_key, factor), -1e30)
    prompt_scores = head_scores(query_block, full_key, factor)
    row_peak = jnp.maximum(jnp.max(near_scores, axis=-1), jnp.max(prompt_scores, axis=-1))
    near_exp = jnp.exp(near_scores - row_peak[..., None])
    prompt_exp = jnp.exp(prompt_scores - row_peak[..., None])
    row_total = jnp.sum(near_exp, axis=-1) + jnp.sum(prompt_exp, axis=-1)
    near_soft = near_exp / row_total[..., None]
    prompt_soft = prompt_exp / row_total[..., None]
    attended = jnp.einsum(
        "hgbk,khd->bhgd",
        near_soft.astype(jnp.bfloat16),
        near_value,
        preferred_element_type=jnp.float32,
    )
    attended = attended + jnp.einsum(
        "hgbk,khd->bhgd",
        prompt_soft.astype(jnp.bfloat16),
        full_value,
        preferred_element_type=jnp.float32,
    )
    row_delta = jnp.transpose(
        jnp.sum(gradient_rows.astype(jnp.float32) * attended, axis=-1), (1, 2, 0)
    )
    near_query, near_kgrad, near_vgrad = block_backward(
        query_block, gradient_rows, near_key, near_value, near_soft, row_delta, factor
    )
    grad_resp_key = near_kgrad.reshape(tok_rows, own_cols).astype(jnp.bfloat16)
    grad_resp_value = near_vgrad.reshape(tok_rows, own_cols).astype(jnp.bfloat16)

    def prompt_block(begin_row, number):
        key_row_block = lax.dynamic_slice_in_dim(full_key, begin_row, number, 0)
        value_row_block = lax.dynamic_slice_in_dim(full_value, begin_row, number, 0)
        soft_rows = lax.dynamic_slice_in_dim(prompt_soft, begin_row, number, 3)
        return block_backward(
            query_block, gradient_rows, key_row_block, value_row_block, soft_rows, row_delta, factor
        )

    def prefix_step(running, index):
        pieces = prompt_block(index * block_rows, block_rows)
        return (running + pieces[0], (pieces[1], pieces[2]))

    query_total, (key_terms, value_terms) = lax.scan(
        prefix_step, near_query, jnp.arange(block_count, dtype=jnp.int32)
    )
    key_sum, value_sum = (
        lax.psum_scatter(
            key_terms.reshape(prompt_len, own_cols), "resp", scatter_dimension=0, tiled=True
        ),
        lax.psum_scatter(
            value_terms.reshape(prompt_len, own_cols), "resp", scatter_dimension=0, tiled=True
        ),
    )
    grad_prompt_key, grad_prompt_value = (
        lax.all_to_all(key_sum, "kvh", split_axis=0, concat_axis=1, tiled=True),
        lax.all_to_all(value_sum, "kvh", split_axis=0, concat_axis=1, tiled=True),
    )
    grad_query = query_total.reshape(tok_rows, heads_here * query_group * HEAD_SIZE).astype(
        jnp.bfloat16
    )
    return (grad_query, grad_resp_key, grad_resp_value, grad_prompt_key, grad_prompt_value)


def solution(mesh):
    return jax.shard_map(
        on_device,
        mesh=mesh,
        in_specs=(
            P("resp", "kvh"),
            P("resp", "kvh"),
            P("resp", "kvh"),
            P(("resp", "kvh"), None),
            P(("resp", "kvh"), None),
            P("resp", "kvh"),
            P("resp", None),
            P("resp", None),
        ),
        out_specs=(
            P("resp", "kvh"),
            P("resp", "kvh"),
            P("resp", "kvh"),
            P(("resp", "kvh"), None),
            P(("resp", "kvh"), None),
        ),
        check_vma=False,
    )
```

profile of v0, /device:TPU:1, one launch (start us, length us, event | category | flops | bytes accessed | tf_op | source)
XLA Modules:
  0.0 1328.8 jit_solution(17140509879586354732)
XLA Ops:
  7.2 11.8 all_to_all.76
  19.0 4.0 all-to-all-start.1
  32.4 240.1 %all-gather.3.cloned.1.call-done = bf16[2048,256]{1,0:T(8,128)(2,1)} async-done(((bf16[32,256]{1,0:T(8,128)(2,1)}), bf16[2048,256]{1,0:T(8,128)(2,1)}) %all-gather.3.cloned.1.call-update) | async-done | bytes 1048592 | tf_op jit(solution)/shard_map/all_gather | solution.py:66
  273.9 2.9 bitcast_reduce_fusion
  277.5 3.5 fusion.15
  281.0 8.2 fusion.14
  289.2 279.7 %all-gather.5.cloned.1.call-done = bf16[2048,256]{1,0:T(8,128)(2,1)} async-done(((bf16[32,256]{1,0:T(8,128)(2,1)}), bf16[2048,256]{1,0:T(8,128)(2,1)}) %all-gather.5.cloned.1.call-update) | async-done | bytes 1048592 | tf_op jit(solution)/shard_map/all_gather | solution.py:67
  570.4 8.9 fusion.16
  585.9 50.1 %while.14 = (s32[]{:T(128)}, f32[256,2,5,128]{0,3,2,1:T(8,128)S(1)}, f32[4,512,2,128]{3,2,1,0:T(2,128)}, f32[4,512,2,128]{3,2,1,0:T(2,128)}, s32[4]{0:T(128)S(1)...) while((s32[]{:T(128)}, ...), condition=%wide.region_9.10_spmd, body=%wide.region_8.9_spmd.sunk | while | flops 1347747840 | bytes 23998160 | solution.py:115
  587.4 3.6 fusion.72
  591.8 3.3 fusion.74
  599.9 3.6 fusion.72
  604.3 3.3 fusion.74
  612.3 3.6 fusion.72
  616.8 3.3 fusion.74
  624.8 3.6 fusion.72
  629.2 3.3 fusion.74
  636.1 3.1 copy.173
  639.2 3.1 copy.172
  642.4 303.6 %reduce-scatter.3.cloned.1.call-done = f32[32,256]{1,0:T(8,128)} async-done(((f32[2048,256]{1,0:T(8,128)}), f32[32,256]{1,0:T(8,128)}) %reduce-scatter.3.cloned.1.call-update) | async-done | bytes 32784 | tf_op jit(solution)/shard_map/reduce_scatter | solution.py:119
  946.0 55.7 %all-to-all-start.2 = ((f32[4,8,256]{2,1,0:T(8,128)}), f32[4,8,256]{2,1,0:T(8,128)S(1)}, u32[]{:S(2)}, u32[]{:S(2)}) async-start(f32[4,8,256]{2,1,0:T(8,128)} %bitcast.210), calls=%async_computation.3 | async-start | bytes 65536 | tf_op jit(solution)/shard_map/all_to_all | solution.py:127
  1001.7 3.5 fusion.28
  1005.2 254.5 %reduce-scatter.5.cloned.1.call-done = f32[32,256]{1,0:T(8,128)} async-done(((f32[2048,256]{1,0:T(8,128)}), f32[32,256]{1,0:T(8,128)}) %reduce-scatter.5.cloned.1.call-update) | async-done | bytes 32784 | tf_op jit(solution)/shard_map/reduce_scatter | solution.py:122
  1260.3 55.2 %all-to-all-start.3 = ((f32[4,8,256]{2,1,0:T(8,128)}), f32[4,8,256]{2,1,0:T(8,128)}, u32[]{:S(2)}, u32[]{:S(2)}) async-start(f32[4,8,256]{2,1,0:T(8,128)} %bitcast.209), calls=%async_computation.5 | async-start | bytes 65536 | tf_op jit(solution)/shard_map/all_to_all | solution.py:128
  (85 shorter events, 46.4 us)
Async XLA Ops:
  7.2 265.3 %all-gather.3.cloned.1.call-start = ((), (), s32[]{:S(2)}) async-start(), calls=%async_computation.6 | async-start | bytes 1064960 | tf_op jit(solution)/shard_map/all_gather | solution.py:66
  19.0 12.4 all-to-all-start.1
  23.0 545.9 %all-gather.5.cloned.1.call-start = ((), (), s32[]{:S(2)}) async-start(), calls=%async_computation.7 | async-start | bytes 1064960 | tf_op jit(solution)/shard_map/all_gather | solution.py:67
  28.3 2.7 copy-start.8
  31.0 1.4 copy-start.6
  31.5 0.6 copy-start.12
  32.1 913.9 %reduce-scatter.3.cloned.1.call-start = ((), (), s32[]{:S(2)}) async-start(), calls=%async_computation.8 | async-start | bytes 2129920 | tf_op jit(solution)/shard_map/reduce_scatter | solution.py:119
  273.9 3.0 copy-start
  273.9 3.0 copy-start.2
  570.4 8.9 copy-start.1
  570.4 8.9 copy-start.3
  570.4 8.9 copy-start.7
  581.4 1.0 copy-start.4
  639.2 620.5 %reduce-scatter.5.cloned.1.call-start = ((), (), s32[]{:S(2)}) async-start(), calls=%async_computation.9 | async-start | bytes 2129920 | tf_op jit(solution)/shard_map/reduce_scatter | solution.py:122
  946.0 313.7 %all-to-all-start.2 = ((f32[4,8,256]{2,1,0:T(8,128)}), f32[4,8,256]{2,1,0:T(8,128)S(1)}, u32[]{:S(2)}, u32[]{:S(2)}) async-start(f32[4,8,256]{2,1,0:T(8,128)} %bitcast.210), calls=%async_computation.3 | async-start | bytes 65536 | tf_op jit(solution)/shard_map/all_to_all | solution.py:127
  1001.7 313.8 %copy-start.5 = (bf16[2,5,256,256]{2,3,1,0:T(8,128)(2,1)S(1)}, bf16[2,5,256,256]{2,3,1,0:T(8,128)(2,1)}, u32[]{:S(2)}) copy-start(bf16[2,5,256,256]{2,3,1,0:T(8,128)(2,1)} %copy-done.4) | copy-start | bytes 3932164
  1259.7 0.6 copy-start.10
  1260.3 59.9 %all-to-all-start.3 = ((f32[4,8,256]{2,1,0:T(8,128)}), f32[4,8,256]{2,1,0:T(8,128)}, u32[]{:S(2)}, u32[]{:S(2)}) async-start(f32[4,8,256]{2,1,0:T(8,128)} %bitcast.209), calls=%async_computation.5 | async-start | bytes 65536 | tf_op jit(solution)/shard_map/all_to_all | solution.py:128
  1315.5 1.7 copy-start.9
  1316.0 4.2 copy-start.11
Sparse Core Ops, SparseCore 0:
  19.2 253.2 all-gather.2
  274.8 294.0 all-gather.4
  639.3 306.6 reduce-scatter.2
  948.5 311.1 reduce-scatter.4
where the time goes:
time: 1330 us
  waiting for transfers between devices  1080 us (81%)
  starting transfers between devices  115 us (9%)
  matrix products  59.3 us (4%)
  local copies, waits for them, and re-layouts  30.7 us (2%)
  other arithmetic  15.4 us (1%)
  between operations  14.1 us (1%)
    reduce_scatter x1, waiting for transfers between devices, on_device(): lax.psum_scatter(key_terms.reshape(prompt_len, own_cols), 'resp', scatter...  304 us
    all_gather x1, waiting for transfers between devices, on_device(): lax.all_gather(head_value, 'resp', axis=0, tiled=True)  280 us
    reduce_scatter x1, waiting for transfers between devices, on_device(): lax.psum_scatter(value_terms.reshape(prompt_len, own_cols), 'resp', scatt...  254 us
    all_gather x1, waiting for transfers between devices, on_device(): lax.all_gather(head_key, 'resp', axis=0, tiled=True)  240 us
    all_to_all x1, starting transfers between devices, on_device(): lax.all_to_all(key_sum, 'kvh', split_axis=0, concat_axis=1, tiled=True)  55.7 us
    all_to_all x1, starting transfers between devices, on_device(): lax.all_to_all(value_sum, 'kvh', split_axis=0, concat_axis=1, tiled=True)  55.2 us
  transfers between devices with their start and end apart: 7, of which 5 were waited for; matrix products, arithmetic and copies ran while one was open for 3% of the time, Pallas kernels for 0%

commit v1 on v0

v1 whole, which is shorter than its diff:
```python
import functools
import math

import jax
import jax.numpy as jnp
from jax import lax
from jax.experimental import pallas as pl
from jax.experimental.pallas import tpu as pltpu
from jax.sharding import Mesh
from jax.sharding import PartitionSpec as P

QUERY_HEADS = 40
KEY_VALUE_HEADS = 8
HEAD = 128
GROUP = QUERY_HEADS // KEY_VALUE_HEADS
CHUNK = 256
LOG2E = 1.4426950408889634

NT = (((1,), (1,)), ((), ()))
NN = (((1,), (0,)), ((), ()))


def dot(a, b, dims):
    return lax.dot_general(a, b, dims, preferred_element_type=jnp.float32)


def attention_kernel(
    len_ref, adv_ref, q_ref, og_ref, nk_ref, nv_ref, kv_ref,
    gq_ref, gnk_ref, gnv_ref, gkv_ref,
    s_ref, dp_ref, acc_ref, kt_ref,
):
    g = pl.program_id(1)
    tokens = q_ref.shape[0]
    prompt = kv_ref.shape[0]
    chunks = prompt // CHUNK
    factor = 1.0 / math.sqrt(HEAD)
    responses = len_ref.shape[1]

    ends = []
    total = 0
    for r in range(responses):
        total = total + len_ref[0, r]
        ends.append(total)

    def segment(pos):
        seg = jnp.zeros(pos.shape, jnp.int32)
        for end in ends:
            seg = seg + (pos >= end).astype(jnp.int32)
        return seg

    tok = lax.broadcasted_iota(jnp.int32, (tokens, HEAD), 0)
    tok_seg = segment(tok)
    weight = jnp.zeros((tokens, HEAD), jnp.float32)
    for r in range(responses):
        weight = jnp.where(tok_seg == r, adv_ref[0, r], weight)

    q = q_ref[...]
    do = (weight * og_ref[...].astype(jnp.float32)).astype(jnp.bfloat16)

    @pl.when(g == 0)
    def _():
        acc_ref[...] = jnp.zeros_like(acc_ref)
        for c in range(chunks):
            kt_ref[:, c * CHUNK:(c + 1) * CHUNK] = (
                kv_ref[c * CHUNK:(c + 1) * CHUNK, :HEAD].astype(jnp.float32).T.astype(jnp.bfloat16)
            )
        kt_ref[:, prompt:] = nk_ref[...].astype(jnp.float32).T.astype(jnp.bfloat16)

    def rows(c):
        return slice(c * CHUNK, (c + 1) * CHUNK)

    def keys(c):
        return kv_ref[rows(c), :HEAD] if c < chunks else nk_ref[...]

    def values(c):
        return kv_ref[rows(c), HEAD:] if c < chunks else nv_ref[...]

    peak = jnp.full((1, tokens), -jnp.inf, jnp.float32)
    for c in range(chunks + 1):
        s = dot(keys(c), q, NT)
        if c == chunks:
            u = lax.broadcasted_iota(jnp.int32, (tokens, tokens), 0)
            t = lax.broadcasted_iota(jnp.int32, (tokens, tokens), 1)
            s = jnp.where((segment(u) == segment(t)) & (u <= t), s, -1e30)
        peak = jnp.maximum(peak, jnp.max(s, axis=0, keepdims=True))
        s_ref[rows(c), :] = s
        dp_ref[rows(c), :] = dot(values(c), do, NT)

    scale = factor * LOG2E
    shift = peak * scale
    row_sum = jnp.zeros((1, tokens), jnp.float32)
    weighted = jnp.zeros((1, tokens), jnp.float32)
    for c in range(chunks + 1):
        p = jnp.exp2(s_ref[rows(c), :] * scale - shift)
        s_ref[rows(c), :] = p
        row_sum = row_sum + jnp.sum(p, axis=0, keepdims=True)
        weighted = weighted + jnp.sum(p * dp_ref[rows(c), :], axis=0, keepdims=True)
    inverse = 1.0 / row_sum
    delta = weighted * inverse

    gq = jnp.zeros((HEAD, tokens), jnp.float32)
    for c in range(chunks + 1):
        p = s_ref[rows(c), :] * inverse
        ds = (p * (dp_ref[rows(c), :] - delta)).astype(jnp.bfloat16)
        acc_ref[rows(c), :HEAD] += dot(ds, q, NN)
        acc_ref[rows(c), HEAD:] += dot(p.astype(jnp.bfloat16), do, NN)
        gq = gq + dot(kt_ref[:, rows(c)], ds, NN)
    gq_ref[...] = (gq.T * factor).astype(jnp.bfloat16)

    @pl.when(g == GROUP - 1)
    def _():
        for c in range(chunks):
            gkv_ref[rows(c), :HEAD] = (acc_ref[rows(c), :HEAD] * factor).astype(jnp.bfloat16)
            gkv_ref[rows(c), HEAD:] = acc_ref[rows(c), HEAD:].astype(jnp.bfloat16)
        gnk_ref[...] = (acc_ref[prompt:, :HEAD] * factor).astype(jnp.bfloat16)
        gnv_ref[...] = acc_ref[prompt:, HEAD:].astype(jnp.bfloat16)


def attention(query, near_key, near_value, kv, out_grad, lengths, advantage):
    tokens = query.shape[0]
    prompt = kv.shape[0]
    heads = near_key.shape[1] // HEAD
    span = prompt + tokens
    smem = pl.BlockSpec(memory_space=pltpu.SMEM)
    by_query = pl.BlockSpec((tokens, HEAD), lambda h, g: (0, h * GROUP + g))
    by_head = pl.BlockSpec((tokens, HEAD), lambda h, g: (0, h))
    by_pair = pl.BlockSpec((prompt, 2 * HEAD), lambda h, g: (0, h))
    return pl.pallas_call(
        attention_kernel,
        grid=(heads, GROUP),
        in_specs=[smem, smem, by_query, by_query, by_head, by_head, by_pair],
        out_specs=[by_query, by_head, by_head, by_pair],
        out_shape=[
            jax.ShapeDtypeStruct(query.shape, jnp.bfloat16),
            jax.ShapeDtypeStruct(near_key.shape, jnp.bfloat16),
            jax.ShapeDtypeStruct(near_key.shape, jnp.bfloat16),
            jax.ShapeDtypeStruct(kv.shape, jnp.bfloat16),
        ],
        scratch_shapes=[
            pltpu.VMEM((span, tokens), jnp.float32),
            pltpu.VMEM((span, tokens), jnp.float32),
            pltpu.VMEM((span, 2 * HEAD), jnp.float32),
            pltpu.VMEM((HEAD, span), jnp.bfloat16),
        ],
        compiler_params=pltpu.CompilerParams(
            dimension_semantics=("arbitrary", "arbitrary"),
            vmem_limit_bytes=48 * 1024 * 1024,
        ),
        cost_estimate=pl.CostEstimate(
            flops=2 * 6 * heads * GROUP * tokens * span * HEAD,
            bytes_accessed=8 * 1024 * 1024,
            transcendentals=heads * GROUP * tokens * span,
        ),
        name="attention",
    )(lengths, advantage, query, out_grad, near_key, near_value, kv)


NEAR = ("z", "kvh")
FAR = ("x", "y")


def exchange(a, axes):
    return lax.all_to_all(a, axes, split_axis=0, concat_axis=0, tiled=True)


def on_device(
    shape, query, response_keys, response_values, prompt_key, prompt_values, out_grad, lengths,
    advantage
):
    x, y, z, kvh = shape
    own = prompt_key.shape[0]
    heads = response_keys.shape[1] // HEAD
    cols = 2 * heads * HEAD
    pairs = jnp.stack(
        [
            prompt_key.reshape(own, kvh, heads, HEAD),
            prompt_values.reshape(own, kvh, heads, HEAD),
        ],
        axis=3,
    ).reshape(own, kvh, cols)
    pairs = jnp.transpose(pairs, (1, 0, 2))
    sent = jnp.broadcast_to(pairs[None], (z, kvh, own, cols)).reshape(z * kvh * own, cols)
    block = exchange(sent, NEAR)
    rows = block.shape[0]
    kv = exchange(jnp.broadcast_to(block[None], (x * y, rows, cols)).reshape(x * y * rows, cols), FAR)

    grad_query, grad_resp_key, grad_resp_value, grad_kv = attention(
        query, response_keys, response_values, kv, out_grad, lengths, advantage
    )

    part = exchange(grad_kv, FAR).reshape(x * y, rows, cols)
    part = jnp.sum(part.astype(jnp.float32), axis=0).astype(jnp.bfloat16)
    part = exchange(part, NEAR).reshape(z, kvh, own, cols)
    grads = jnp.sum(part.astype(jnp.float32), axis=0).reshape(kvh, own, heads, 2, HEAD)
    grads = jnp.transpose(grads, (3, 1, 0, 2, 4)).reshape(2, own, kvh * heads * HEAD)
    return (grad_query, grad_resp_key, grad_resp_value, grads[0], grads[1])


def solution(mesh):
    x, y, z, kvh = 4, 2, 8, 4
    fine = Mesh(mesh.devices.reshape(x, y, z, kvh), ("x", "y", "z", "kvh"))
    resp = ("x", "y", "z")
    every = ("x", "y", "z", "kvh")
    return jax.shard_map(
        functools.partial(on_device, (x, y, z, kvh)),
        mesh=fine,
        in_specs=(
            P(resp, "kvh"),
            P(resp, "kvh"),
            P(resp, "kvh"),
            P(every, None),
            P(every, None),
            P(resp, "kvh"),
            P(resp, None),
            P(resp, None),
        ),
        out_specs=(
            P(resp, "kvh"),
            P(resp, "kvh"),
            P(resp, "kvh"),
            P(every, None),
            P(every, None),
        ),
        check_vma=False,
    )
```

time: 1330 us -> 141 us (0.11)
  waiting for transfers between devices: 1080 us -> 0 us
  starting transfers between devices: 115 us -> 0 us
  blocking collectives: 11.8 us -> 103 us
  matrix products: 59.3 us -> 0 us
  Pallas kernels: 0 us -> 33.6 us
  local copies, waits for them, and re-layouts: 30.7 us -> 2.37 us
  other arithmetic: 15.4 us -> 0.51 us
  between operations: 14.1 us -> 0.75 us
    reduce_scatter x2 -> x0, waiting for transfers between devices: 558 us -> none  [the longest x1 304 us: on_device(): lax.psum_scatter(key_terms.reshape(prompt_len, own_cols), 'resp', scatter...]
    all_gather x2 -> x0, waiting for transfers between devices: 520 us -> none  [the longest x1 280 us: on_device(): lax.all_gather(head_value, 'resp', axis=0, tiled=True)]
    all_to_all x3 -> x0, starting transfers between devices: 115 us -> none  [the longest x1 55.7 us: on_device(): lax.all_to_all(key_sum, 'kvh', split_axis=0, concat_axis=1, tiled=True)]
    all_to_all x1 -> x4, blocking collectives: 11.8 us -> 103 us  [exchange(): return lax.all_to_all(a, axes, split_axis=0, concat_axis=0, tiled=True)]
    dot_general x24 -> x0, matrix products: 59.3 us -> none  [the longest x5 16.8 us: block_backward(): jnp.einsum('rlev,erlp->vrp', rounded_length, gradient_rows, preferred_ele...]
    pallas_call x0 -> x1, Pallas kernels: none -> 33.6 us  [attention(): pl.pallas_call(attention_kernel, grid=(heads, GROUP), in_specs=[smem, sme...]
    unnamed x34 -> x12, local copies, waits for them, and re-layouts: 14.4 us -> 0.04 us
  transfers between devices with their start and end apart: 7 -> 0, of which waited for: 5 -> 0; matrix products, arithmetic and copies ran while one was open for 3% -> 0% of each run, Pallas kernels for 0% -> 0%
where the time goes in v1:
time: 141 us; the launch traced here: 140 us
  blocking collectives  103 us (73%)
  Pallas kernels  33.6 us (24%)
  local copies, waits for them, and re-layouts  2.37 us (2%)
    all_to_all x4, blocking collectives, exchange(): return lax.all_to_all(a, axes, split_axis=0, concat_axis=0, tiled=True)  103 us
    pallas_call x1, Pallas kernels, attention(): pl.pallas_call(attention_kernel, grid=(heads, GROUP), in_specs=[smem, sme...  33.6 us

profile of v1, /device:TPU:1, one launch (start us, length us, event | category | flops | bytes accessed | tf_op | source)
XLA Modules:
  0.0 140.3 jit_solution(7014468255803410508)
XLA Ops:
  0.6 0.7 copy.15
  1.4 0.7 copy.16
  2.1 0.1 pad_maximum_fusion
  2.3 25.5 %all_to_all.35 = bf16[32,8,512]{2,1,0:T(8,128)(2,1)S(1)} all-to-all(bf16[32,8,512]{2,1,0:T(8,128)(2,1)S(1)} %bitcast.22), channel_id=1, replica_groups=mesh['x'=4,'y'=2,'z'=8,'kvh'=4] {'z','kvh'}, dimensions={0} | all-to-all | bytes 524288 | tf_op jit(solution)/shard_map/all_to_all | solution.py:163
  27.8 0.2 broadcast_in_dim.16
  27.9 0.0 copy-start
  28.0 0.0 copy-start.1
  28.0 0.0 copy-start.2
  28.0 0.0 copy-start.3
  28.0 0.0 copy-start.4
  28.0 0.0 copy-start.5
  28.0 29.5 %all_to_all.36 = bf16[8,256,512]{2,1,0:T(8,128)(2,1)S(1)} all-to-all(bf16[8,256,512]{2,1,0:T(8,128)(2,1)S(1)} %broadcast_in_dim.16), channel_id=1, replica_groups=mesh['x'=4,'y'=2,'z'=8,'kvh'=4] {'x','y'}, dimensions={0} | all-to-all | bytes 4194304 | tf_op jit(solution)/shard_map/all_to_all | solution.py:163
  57.5 0.0 copy-done
  57.5 0.0 copy-done.1
  57.5 0.0 copy-done.2
  57.5 0.0 copy-done.3
  57.5 0.0 copy-done.4
  57.6 0.0 copy-done.5
  57.6 33.6 %attention.1 = (bf16[256,1280]{1,0:T(8,128)(2,1)}, bf16[256,256]{1,0:T(8,128)(2,1)}, bf16[256,256]{1,0:T(8,128)(2,1)}, bf16[2048,512]{1,0:T(8,128)(2,1)S(1)}) custom-call(s32[1,2]{1,0:T(1,128)S(1)} %copy-done.4, f32[1,2]{1,0:T(1,128)S(1)} %copy-done.5, bf16[256,1280]{1,0:T(8,128)(2,1)S(1)} %copy-done, bf16[256,1280]{1,0:T(8,128)(2,1)S(1)} %copy-done.1, ...), custom_call_target="tpu_custom_call" | custom-call | flops 9059696640 | bytes 8388608 | tf_op jit(solution)/shard_map/attention/pallas_call | solution.py:128
  91.2 28.4 %all_to_all.37 = bf16[8,256,512]{2,1,0:T(8,128)(2,1)S(1)} all-to-all(bf16[8,256,512]{2,1,0:T(8,128)(2,1)S(1)} %bitcast.18), channel_id=1, replica_groups=mesh['x'=4,'y'=2,'z'=8,'kvh'=4] {'x','y'}, dimensions={0} | all-to-all | bytes 4194304 | tf_op jit(solution)/shard_map/all_to_all | solution.py:163
  119.6 0.4 reduce_sum.21
  120.0 19.6 %all_to_all.38 = bf16[32,8,512]{2,1,0:T(8,128)(2,1)S(1)} all-to-all(bf16[32,8,512]{2,1,0:T(8,128)(2,1)S(1)} %bitcast.19), channel_id=1, replica_groups=mesh['x'=4,'y'=2,'z'=8,'kvh'=4] {'z','kvh'}, dimensions={0} | all-to-all | bytes 524288 | tf_op jit(solution)/shard_map/all_to_all | solution.py:163
  139.6 0.6 fusion
  (3 shorter events, 0.1 us)
Async XLA Ops:
  27.9 29.6 %copy-start = (bf16[256,1280]{1,0:T(8,128)(2,1)S(1)}, bf16[256,1280]{1,0:T(8,128)(2,1)}, u32[]{:S(2)}) copy-start(bf16[256,1280]{1,0:T(8,128)(2,1)} %q_ref.1) | copy-start | bytes 1966084
  28.0 29.6 %copy-start.1 = (bf16[256,1280]{1,0:T(8,128)(2,1)S(1)}, bf16[256,1280]{1,0:T(8,128)(2,1)}, u32[]{:S(2)}) copy-start(bf16[256,1280]{1,0:T(8,128)(2,1)} %og_ref.1) | copy-start | bytes 1966084
  28.0 29.6 %copy-start.2 = (bf16[256,256]{1,0:T(8,128)(2,1)S(1)}, bf16[256,256]{1,0:T(8,128)(2,1)}, u32[]{:S(2)}) copy-start(bf16[256,256]{1,0:T(8,128)(2,1)} %nk_ref.1) | copy-start | bytes 393220
  28.0 29.6 %copy-start.3 = (bf16[256,256]{1,0:T(8,128)(2,1)S(1)}, bf16[256,256]{1,0:T(8,128)(2,1)}, u32[]{:S(2)}) copy-start(bf16[256,256]{1,0:T(8,128)(2,1)} %nv_ref.1) | copy-start | bytes 393220
  28.0 29.6 %copy-start.4 = (s32[1,2]{1,0:T(1,128)S(1)}, s32[1,2]{1,0:T(1,128)}, u32[]{:S(2)}) copy-start(s32[1,2]{1,0:T(1,128)} %len_ref.1) | copy-start | bytes 28
  28.0 29.6 %copy-start.5 = (f32[1,2]{1,0:T(1,128)S(1)}, f32[1,2]{1,0:T(1,128)}, u32[]{:S(2)}) copy-start(f32[1,2]{1,0:T(1,128)} %adv_ref.1) | copy-start | bytes 28

commit v2 on v1

--- a/solution.py
+++ b/solution.py
@@ -25,11 +25,10 @@
 
 
 def attention_kernel(
-    len_ref, adv_ref, q_ref, og_ref, nk_ref, nv_ref, kv_ref,
-    gq_ref, gnk_ref, gnv_ref, gkv_ref,
-    s_ref, dp_ref, acc_ref, kt_ref,
+    len_ref, adv_ref, q_ref, og_ref, nk_ref, nv_ref, kv_ref, *rest
 ):
-    g = pl.program_id(1)
+    gq_ref, gnk_ref, gnv_ref, gkv_ref, s_ref, dp_ref, acc_ref, kt_ref = rest[-8:]
+    g = pl.program_id(0)
     tokens = q_ref.shape[0]
     prompt = kv_ref.shape[0]
     chunks = prompt // CHUNK
@@ -116,26 +115,27 @@
         gnv_ref[...] = acc_ref[prompt:, HEAD:].astype(jnp.bfloat16)
 
 
-def attention(query, near_key, near_value, kv, out_grad, lengths, advantage):
+def attention(head, query, near_key, near_value, kv, out_grad, lengths, advantage, before):
     tokens = query.shape[0]
     prompt = kv.shape[0]
-    heads = near_key.shape[1] // HEAD
     span = prompt + tokens
     smem = pl.BlockSpec(memory_space=pltpu.SMEM)
-    by_query = pl.BlockSpec((tokens, HEAD), lambda h, g: (0, h * GROUP + g))
-    by_head = pl.BlockSpec((tokens, HEAD), lambda h, g: (0, h))
-    by_pair = pl.BlockSpec((prompt, 2 * HEAD), lambda h, g: (0, h))
+    by_query = pl.BlockSpec((tokens, HEAD), lambda g: (0, head * GROUP + g))
+    by_head = pl.BlockSpec((tokens, HEAD), lambda g: (0, head))
+    whole = pl.BlockSpec((prompt, 2 * HEAD), lambda g: (0, 0))
     return pl.pallas_call(
         attention_kernel,
-        grid=(heads, GROUP),
-        in_specs=[smem, smem, by_query, by_query, by_head, by_head, by_pair],
-        out_specs=[by_query, by_head, by_head, by_pair],
+        grid=(GROUP,),
+        in_specs=[smem, smem, by_query, by_query, by_head, by_head, whole]
+        + [pl.BlockSpec(memory_space=pl.ANY)] * len(before),
+        out_specs=[by_query, by_head, by_head, whole],
         out_shape=[
             jax.ShapeDtypeStruct(query.shape, jnp.bfloat16),
             jax.ShapeDtypeStruct(near_key.shape, jnp.bfloat16),
             jax.ShapeDtypeStruct(near_key.shape, jnp.bfloat16),
             jax.ShapeDtypeStruct(kv.shape, jnp.bfloat16),
         ],
+        input_output_aliases={7 + i: i for i in range(len(before))},
         scratch_shapes=[
             pltpu.VMEM((span, tokens), jnp.float32),
             pltpu.VMEM((span, tokens), jnp.float32),
@@ -143,20 +143,20 @@
             pltpu.VMEM((HEAD, span), jnp.bfloat16),
         ],
         compiler_params=pltpu.CompilerParams(
-            dimension_semantics=("arbitrary", "arbitrary"),
-            vmem_limit_bytes=48 * 1024 * 1024,
+            dimension_semantics=("arbitrary",),
+            vmem_limit_bytes=40 * 1024 * 1024,
         ),
         cost_estimate=pl.CostEstimate(
-            flops=2 * 6 * heads * GROUP * tokens * span * HEAD,
-            bytes_accessed=8 * 1024 * 1024,
-            transcendentals=heads * GROUP * tokens * span,
+            flops=2 * 6 * GROUP * tokens * span * HEAD,
+            bytes_accessed=4 * 1024 * 1024,
+            transcendentals=GROUP * tokens * span,
         ),
         name="attention",
-    )(lengths, advantage, query, out_grad, near_key, near_value, kv)
-
-
-NEAR = ("z", "kvh")
-FAR = ("x", "y")
+    )(lengths, advantage, query, out_grad, near_key, near_value, kv, *before)
+
+
+NEAR = ("zh", "kvh")
+FAR = ("x", "y", "zl")
 
 
 def exchange(a, axes):
@@ -167,7 +167,8 @@
     shape, query, response_keys, response_values, prompt_key, prompt_values, out_grad, lengths,
     advantage
 ):
-    x, y, z, kvh = shape
+    x, y, zh, zl, kvh = shape
+    far = x * y * zl
     own = prompt_key.shape[0]
     heads = response_keys.shape[1] // HEAD
     cols = 2 * heads * HEAD
@@ -179,37 +180,44 @@
         axis=3,
     ).reshape(own, kvh, cols)
     pairs = jnp.transpose(pairs, (1, 0, 2))
-    sent = jnp.broadcast_to(pairs[None], (z, kvh, own, cols)).reshape(z * kvh * own, cols)
+    sent = jnp.broadcast_to(pairs[None], (zh, kvh, own, cols)).reshape(zh * kvh * own, cols)
     block = exchange(sent, NEAR)
     rows = block.shape[0]
-    kv = exchange(jnp.broadcast_to(block[None], (x * y, rows, cols)).reshape(x * y * rows, cols), FAR)
-
-    grad_query, grad_resp_key, grad_resp_value, grad_kv = attention(
-        query, response_keys, response_values, kv, out_grad, lengths, advantage
-    )
-
-    part = exchange(grad_kv, FAR).reshape(x * y, rows, cols)
-    part = jnp.sum(part.astype(jnp.float32), axis=0).astype(jnp.bfloat16)
-    part = exchange(part, NEAR).reshape(z, kvh, own, cols)
+    wide = 2 * HEAD
+
+    def spread(head):
+        part = block[:, head * wide:(head + 1) * wide]
+        return exchange(jnp.broadcast_to(part[None], (far, rows, wide)).reshape(far * rows, wide), FAR)
+
+    before = ()
+    sums = []
+    for head in range(heads):
+        *before, grad_kv = attention(
+            head, query, response_keys, response_values, spread(head), out_grad, lengths, advantage,
+            before
+        )
+        part = exchange(grad_kv, FAR).reshape(far, rows, wide)
+        sums.append(jnp.sum(part.astype(jnp.float32), axis=0).astype(jnp.bfloat16))
+    part = exchange(jnp.concatenate(sums, axis=1), NEAR).reshape(zh, kvh, own, cols)
     grads = jnp.sum(part.astype(jnp.float32), axis=0).reshape(kvh, own, heads, 2, HEAD)
     grads = jnp.transpose(grads, (3, 1, 0, 2, 4)).reshape(2, own, kvh * heads * HEAD)
-    return (grad_query, grad_resp_key, grad_resp_value, grads[0], grads[1])
+    return (*before, grads[0], grads[1])
 
 
 def solution(mesh):
-    x, y, z, kvh = 4, 2, 8, 4
-    fine = Mesh(mesh.devices.reshape(x, y, z, kvh), ("x", "y", "z", "kvh"))
-    resp = ("x", "y", "z")
-    every = ("x", "y", "z", "kvh")
+    shape = (4, 2, 4, 2, 4)
+    names = ("x", "y", "zh", "zl", "kvh")
+    fine = Mesh(mesh.devices.reshape(shape), names)
+    resp = names[:4]
     return jax.shard_map(
-        functools.partial(on_device, (x, y, z, kvh)),
+        functools.partial(on_device, shape),
         mesh=fine,
         in_specs=(
             P(resp, "kvh"),
             P(resp, "kvh"),
             P(resp, "kvh"),
-            P(every, None),
-            P(every, None),
+            P(names, None),
+            P(names, None),
             P(resp, "kvh"),
             P(resp, None),
             P(resp, None),
@@ -218,8 +226,8 @@
             P(resp, "kvh"),
             P(resp, "kvh"),
             P(resp, "kvh"),
-            P(every, None),
-            P(every, None),
+            P(names, None),
+            P(names, None),
         ),
         check_vma=False,
     )

time: 141 us -> 131 us (0.929)
  blocking collectives: 103 us -> 60.5 us
  starting transfers between devices: 0 us -> 16 us
  waiting for transfers between devices: 0 us -> 12.3 us
  local copies, waits for them, and re-layouts: 2.37 us -> 4.21 us
  Pallas kernels: 33.6 us -> 35.1 us
    all_to_all x4 -> x3, blocking collectives: 103 us -> 60.5 us  [exchange(): return lax.all_to_all(a, axes, split_axis=0, concat_axis=0, tiled=True)]
    all_to_all x0 -> x3, starting transfers between devices: none -> 16 us  [exchange(): return lax.all_to_all(a, axes, split_axis=0, concat_axis=0, tiled=True)]
    all_to_all x0 -> x3, waiting for transfers between devices: none -> 12.3 us  [exchange(): return lax.all_to_all(a, axes, split_axis=0, concat_axis=0, tiled=True)]
    unnamed x12 -> x16, local copies, waits for them, and re-layouts: 0.04 us -> 1.55 us
    pallas_call x1 -> x2, Pallas kernels: 33.6 us -> 35.1 us  [attention(): pl.pallas_call(attention_kernel, grid=(GROUP,), in_specs=[smem, smem, by_...]
  transfers between devices with their start and end apart: 0 -> 3, of which waited for: 0 -> 1; matrix products, arithmetic and copies ran while one was open for 0% -> 1% of each run, Pallas kernels for 0% -> 27%
where the time goes in v2:
time: 131 us; the launch traced here: 130 us
  blocking collectives  60.5 us (46%)
  Pallas kernels  35.1 us (27%)
  starting transfers between devices  16 us (12%)
  waiting for transfers between devices  12.3 us (9%)
  local copies, waits for them, and re-layouts  4.21 us (3%)
  other arithmetic  1.63 us (1%)
    all_to_all x3, blocking collectives, exchange(): return lax.all_to_all(a, axes, split_axis=0, concat_axis=0, tiled=True)  60.5 us
    pallas_call x2, Pallas kernels, attention(): pl.pallas_call(attention_kernel, grid=(GROUP,), in_specs=[smem, smem, by_...  35.1 us
    all_to_all x3, starting transfers between devices, exchange(): return lax.all_to_all(a, axes, split_axis=0, concat_axis=0, tiled=True)  16 us
    all_to_all x3, waiting for transfers between devices, exchange(): return lax.all_to_all(a, axes, split_axis=0, concat_axis=0, tiled=True)  12.3 us
  transfers between devices with their start and end apart: 3, of which 1 were waited for; matrix products, arithmetic and copies ran while one was open for 1% of the time, Pallas kernels for 27%

profile of v2, /device:TPU:1, one launch (start us, length us, event | category | flops | bytes accessed | tf_op | source)
XLA Modules:
  0.0 130.5 jit_solution(16626409188569757269)
XLA Ops:
  0.6 0.0 copy-start.7
  0.6 0.7 copy.18
  1.4 0.1 pad_maximum_fusion
  1.6 23.4 %all_to_all.55 = bf16[16,8,512]{2,1,0:T(8,128)(2,1)S(1)} all-to-all(bf16[16,8,512]{2,1,0:T(8,128)(2,1)S(1)} %bitcast.22), channel_id=1, replica_groups=mesh['x'=4,'y'=2,'zh'=4,'zl'=2,'kvh'=4] {'zh','kvh'}, dimensions={0} | all-to-all | bytes 262144 | tf_op jit(solution)/shard_map/all_to_all | solution.py:163
  24.9 0.1 broadcast_in_dim.8
  25.0 20.5 %all_to_all.56 = bf16[16,128,256]{2,1,0:T(8,128)(2,1)S(1)} all-to-all(bf16[16,128,256]{2,1,0:T(8,128)(2,1)S(1)} %broadcast_in_dim.8), channel_id=1, replica_groups=mesh['x'=4,'y'=2,'zh'=4,'zl'=2,'kvh'=4] {'x','y','zl'}, dimensions={0} | all-to-all | bytes 2097152 | tf_op jit(solution)/shard_map/all_to_all | solution.py:163
  45.5 1.1 broadcast_in_dim.7
  46.7 3.8 %all-to-all-start.1 = ((bf16[16,128,256]{2,1,0:T(8,128)(2,1)}), bf16[16,128,256]{2,1,0:T(8,128)(2,1)S(1)}, u32[]{:S(2)}, u32[]{:S(2)}) async-start(bf16[16,128,256]{2,1,0:T(8,128)(2,1)} %broadcast_in_dim.7), calls=%async_computation.1 | async-start | bytes 2097152 | tf_op jit(solution)/shard_map/all_to_all | solution.py:163
  50.5 0.0 copy-start.5
  50.5 0.0 copy-start.6
  50.5 0.6 copy-done.5
  51.1 0.0 copy-done.6
  51.1 0.9 copy-done.3
  52.0 17.5 %attention.2 = (bf16[256,1280]{1,0:T(8,128)(2,1)}, bf16[256,256]{1,0:T(8,128)(2,1)}, bf16[256,256]{1,0:T(8,128)(2,1)}, bf16[2048,256]{1,0:T(8,128)(2,1)}) custom-call(s32[1,2]{1,0:T(1,128)S(1)} %copy-done.5, f32[1,2]{1,0:T(1,128)S(1)} %copy-done.6, bf16[256,1280]{1,0:T(8,128)(2,1)S(1)} %copy-done, bf16[256,1280]{1,0:T(8,128)(2,1)S(1)} %copy-done.1, ...), custom_call_target="tpu_custom_call" | custom-call | flops 4529848320 | bytes 4194304 | tf_op jit(solution)/shard_map/attention/pallas_call | solution.py:126
  69.5 0.0 all-to-all-done.1
  69.6 6.2 %all-to-all-start.3 = ((bf16[16,128,256]{2,1,0:T(8,128)(2,1)}), bf16[16,128,256]{2,1,0:T(8,128)(2,1)}, u32[]{:S(2)}, u32[]{:S(2)}) async-start(bf16[16,128,256]{2,1,0:T(8,128)(2,1)} %bitcast.7), calls=%async_computation.3 | async-start | bytes 2097152 | tf_op jit(solution)/shard_map/all_to_all | solution.py:163
  75.7 17.6 %attention.3 = (bf16[256,1280]{1,0:T(8,128)(2,1)}, bf16[256,256]{1,0:T(8,128)(2,1)}, bf16[256,256]{1,0:T(8,128)(2,1)}, bf16[2048,256]{1,0:T(8,128)(2,1)}) custom-call(s32[1,2]{1,0:T(1,128)S(1)} %copy-done.5, f32[1,2]{1,0:T(1,128)S(1)} %copy-done.6, bf16[256,1280]{1,0:T(8,128)(2,1)S(1)} %copy-done, ...), custom_call_target="tpu_custom_call", output_to_operand_aliasing={{0}: (7, {}), {1}: (8, {}), {2}: (9, {})} | custom-call | flops 4529848320 | bytes 4194304 | tf_op jit(solution)/shard_map/attention/pallas_call | solution.py:126
  93.3 0.0 all-to-all-done.3
  93.3 6.0 %all-to-all-start.4 = ((bf16[16,128,256]{2,1,0:T(8,128)(2,1)}), bf16[16,128,256]{2,1,0:T(8,128)(2,1)S(1)}, u32[]{:S(2)}, u32[]{:S(2)}) async-start(bf16[16,128,256]{2,1,0:T(8,128)(2,1)} %bitcast.8), calls=%async_computation.4 | async-start | bytes 2097152 | tf_op jit(solution)/shard_map/all_to_all | solution.py:163
  99.3 1.4 %reduce_sum.33 = bf16[128,256]{1,0:T(8,128)(2,1)S(1)} reduce(bf16[16,128,256]{2,1,0:T(8,128)(2,1)} %all-to-all-done.3, bf16[]{:T(256)} %constant.3.clone.1), dimensions={0}, to_apply=%region_0.0 | reduce | flops 491520 | bytes 1114114 | tf_op jit(solution)/shard_map/reduce_sum | solution.py:200
  100.7 12.3 %all-to-all-done.4 = bf16[16,128,256]{2,1,0:T(8,128)(2,1)S(1)} async-done(((bf16[16,128,256]{2,1,0:T(8,128)(2,1)}), bf16[16,128,256]{2,1,0:T(8,128)(2,1)S(1)}, u32[]{:S(2)}, u32[]{:S(2)}) %all-to-all-start.4) | async-done | bytes 1048608 | tf_op jit(solution)/shard_map/all_to_all | solution.py:163
  113.0 0.1 reduce_sum.34
  113.2 16.6 %all_to_all.57 = bf16[16,8,512]{2,1,0:T(8,128)(2,1)S(1)} all-to-all(bf16[16,8,512]{2,1,0:T(8,128)(2,1)S(1)} %maximum_bitcast_fusion), channel_id=1, replica_groups=mesh['x'=4,'y'=2,'zh'=4,'zl'=2,'kvh'=4] {'zh','kvh'}, dimensions={0} | all-to-all | bytes 262144 | tf_op jit(solution)/shard_map/all_to_all | solution.py:163
  129.8 0.6 fusion.1
  (16 shorter events, 0.1 us)
Async XLA Ops:
  0.6 0.8 copy-start.7
  46.7 3.8 %copy-start = (bf16[256,1280]{1,0:T(8,128)(2,1)S(1)}, bf16[256,1280]{1,0:T(8,128)(2,1)}, u32[]{:S(2)}) copy-start(bf16[256,1280]{1,0:T(8,128)(2,1)} %q_ref.3) | copy-start | bytes 1966084
  46.7 3.8 %copy-start.1 = (bf16[256,1280]{1,0:T(8,128)(2,1)S(1)}, bf16[256,1280]{1,0:T(8,128)(2,1)}, u32[]{:S(2)}) copy-start(bf16[256,1280]{1,0:T(8,128)(2,1)} %og_ref.3) | copy-start | bytes 1966084
  46.7 3.8 %copy-start.2 = (bf16[256,256]{1,0:T(8,128)(2,1)S(1)}, bf16[256,256]{1,0:T(8,128)(2,1)}, u32[]{:S(2)}) copy-start(bf16[256,256]{1,0:T(8,128)(2,1)} %nk_ref.3) | copy-start | bytes 393220
  46.7 22.9 %all-to-all-start.1 = ((bf16[16,128,256]{2,1,0:T(8,128)(2,1)}), bf16[16,128,256]{2,1,0:T(8,128)(2,1)S(1)}, u32[]{:S(2)}, u32[]{:S(2)}) async-start(bf16[16,128,256]{2,1,0:T(8,128)(2,1)} %broadcast_in_dim.7), calls=%async_computation.1 | async-start | bytes 2097152 | tf_op jit(solution)/shard_map/all_to_all | solution.py:163
  50.5 0.7 copy-start.5
  50.5 0.7 copy-start.6
  51.1 0.9 copy-start.3
  69.6 6.2 %copy-start.4 = (bf16[256,256]{1,0:T(8,128)(2,1)S(1)}, bf16[256,256]{1,0:T(8,128)(2,1)}, u32[]{:S(2)}) copy-start(bf16[256,256]{1,0:T(8,128)(2,1)} %nv_ref.3) | copy-start | bytes 393220
  69.6 23.7 %all-to-all-start.3 = ((bf16[16,128,256]{2,1,0:T(8,128)(2,1)}), bf16[16,128,256]{2,1,0:T(8,128)(2,1)}, u32[]{:S(2)}, u32[]{:S(2)}) async-start(bf16[16,128,256]{2,1,0:T(8,128)(2,1)} %bitcast.7), calls=%async_computation.3 | async-start | bytes 2097152 | tf_op jit(solution)/shard_map/all_to_all | solution.py:163
  93.3 19.7 %all-to-all-start.4 = ((bf16[16,128,256]{2,1,0:T(8,128)(2,1)}), bf16[16,128,256]{2,1,0:T(8,128)(2,1)S(1)}, u32[]{:S(2)}, u32[]{:S(2)}) async-start(bf16[16,128,256]{2,1,0:T(8,128)(2,1)} %bitcast.8), calls=%async_computation.4 | async-start | bytes 2097152 | tf_op jit(solution)/shard_map/all_to_all | solution.py:163

commit v3 on v2

v3 whole, which is shorter than its diff:
```python
import functools
import math

import jax
import jax.numpy as jnp
from jax import lax
from jax.experimental import pallas as pl
from jax.experimental.pallas import tpu as pltpu
from jax.sharding import Mesh
from jax.sharding import PartitionSpec as P

QUERY_HEADS = 40
KEY_VALUE_HEADS = 8
HEAD = 128
GROUP = QUERY_HEADS // KEY_VALUE_HEADS
CHUNK = 1024
FOLD = 16
VMEM_MIB = 38
TIE = True
HALF = (GROUP + 1) * HEAD
Q_COLS = slice(0, GROUP * HEAD)
K_COLS = slice(GROUP * HEAD, HALF)
O_COLS = slice(HALF, HALF + GROUP * HEAD)
V_COLS = slice(HALF + GROUP * HEAD, 2 * HALF)
GK_COLS = slice(GROUP * HEAD, (GROUP + 1) * HEAD)
GV_COLS = slice((GROUP + 1) * HEAD, (GROUP + 2) * HEAD)
LOG2E = 1.4426950408889634

NN = (((1,), (0,)), ((), ()))


def dot(a, b, dims):
    return lax.dot_general(a, b, dims, preferred_element_type=jnp.float32)


def attention_kernel(
    len_ref, adv_ref, got_ref, q_hbm, og_hbm, nk_hbm, nv_hbm, got_a_hbm, got_b_hbm, kv_hbm,
    gq_hbm, gnk_hbm, gnv_hbm, back_hbm, gkv_hbm,
    tok_ref, kv_ref, grad_ref, gkv_ref, sum_kv_ref,
    p_ref, d_ref, kt_ref, qt_ref, dot_t_ref, gqt_ref,
    peak_ref, sum_ref, dot_ref, in_sem, kv_sem, out_sem,
):
    tokens = tok_ref.shape[1]
    prompt = kv_ref.shape[0]
    chunks = prompt // CHUNK
    factor = 1.0 / math.sqrt(HEAD)
    scale = factor * LOG2E

    mine = lax.axis_index("zl")
    query_cols = pl.ds(pl.multiple_of(mine * (GROUP * HEAD), HEAD), GROUP * HEAD)
    own_cols = pl.ds(pl.multiple_of(mine * HEAD, HEAD), HEAD)
    own_loads = [
        pltpu.make_async_copy(q_hbm.at[:, query_cols], tok_ref.at[0, :, Q_COLS], in_sem.at[0]),
        pltpu.make_async_copy(og_hbm.at[:, query_cols], tok_ref.at[0, :, O_COLS], in_sem.at[1]),
        pltpu.make_async_copy(nk_hbm.at[:, own_cols], tok_ref.at[0, :, K_COLS], in_sem.at[2]),
        pltpu.make_async_copy(nv_hbm.at[:, own_cols], tok_ref.at[0, :, V_COLS], in_sem.at[3]),
    ]
    got_loads = [
        pltpu.make_async_copy(got_a_hbm, tok_ref.at[1, :, pl.ds(0, HALF)], in_sem.at[4]),
        pltpu.make_async_copy(got_b_hbm, tok_ref.at[1, :, pl.ds(HALF, HALF)], in_sem.at[5]),
    ]
    for copy in own_loads:
        copy.start()
    kv_loads = []
    for c in range(chunks):
        at = pl.ds(c * CHUNK, CHUNK)
        kv_loads.append(pltpu.make_async_copy(kv_hbm.at[at], kv_ref.at[at], kv_sem.at[c]))
        kv_loads[-1].start()
    for copy in got_loads:
        copy.start()

    responses = len_ref.shape[1]

    def segment(pos, ends):
        seg = jnp.zeros(pos.shape, jnp.int32)
        for end in ends:
            seg = seg + (pos >= end).astype(jnp.int32)
        return seg

    def head_cols(g, first=0):
        return slice(first + g * HEAD, first + (g + 1) * HEAD)

    def tok_cols(g):
        return slice(g * tokens, (g + 1) * tokens)

    def turn(a):
        return a.astype(jnp.float32).T.astype(jnp.bfloat16)

    def forward(keys, values, row, mask):
        size = keys.shape[0]
        groups = size // (8 * FOLD)
        for g in range(GROUP):
            s = dot(keys, qt_ref[:, tok_cols(g)], NN)
            if mask is not None:
                s = jnp.where(mask, s, -1e30)
            d = dot(values, dot_t_ref[:, tok_cols(g)], NN)
            s = s.reshape(groups, FOLD, 8, tokens)
            d_ref[row:row + size, tok_cols(g)] = d
            d = d.reshape(groups, FOLD, 8, tokens)
            for i in range(groups):
                slot = row // FOLD + 8 * i
                key = row + 8 * FOLD * i
                peak = jnp.max(s[i], axis=0)
                e = jnp.exp2((s[i] - peak[None]) * scale)
                p_ref[key:key + 8 * FOLD, tok_cols(g)] = e.reshape(8 * FOLD, tokens)
                peak_ref[slot:slot + 8, tok_cols(g)] = peak
                sum_ref[slot:slot + 8, tok_cols(g)] = jnp.sum(e, axis=0)
                dot_ref[slot:slot + 8, tok_cols(g)] = jnp.sum(e * d[i], axis=0)

    def backward(part, row, size, deltas):
        groups = size // (8 * FOLD)
        slot = row // FOLD
        key_sum = jnp.zeros((size, HEAD), jnp.float32)
        value_sum = jnp.zeros((size, HEAD), jnp.float32)
        for g in range(GROUP):
            p = p_ref[row:row + size, tok_cols(g)].reshape(groups, FOLD, 8, tokens)
            d = d_ref[row:row + size, tok_cols(g)].reshape(groups, FOLD, 8, tokens)
            share = peak_ref[slot:slot + 8 * groups, tok_cols(g)].reshape(groups, 1, 8, tokens)
            p = p * share
            ds = p * (d - deltas[g][None, None])
            p = p.reshape(size, tokens).astype(jnp.bfloat16)
            ds = ds.reshape(size, tokens).astype(jnp.bfloat16)
            key_sum = key_sum + dot(ds, tok_ref[part, :, head_cols(g)], NN)
            value_sum = value_sum + dot(p, tok_ref[part, :, head_cols(g, HALF)], NN)
            query_sum = dot(kt_ref[:, row:row + size], ds, NN)
            if row == 0:
                gqt_ref[:, tok_cols(g)] = query_sum
            else:
                gqt_ref[:, tok_cols(g)] += query_sum
        return key_sum * factor, value_sum

    stores = []

    def store(source, target):
        stores.append(pltpu.make_async_copy(source, target, out_sem.at[len(stores)]))
        stores[-1].start()

    parts = tok_ref.shape[0]
    for part in range(parts):
        if part == 0:
            lengths = [len_ref[0, r] for r in range(responses)]
            advantages = [adv_ref[0, r] for r in range(responses)]
        else:
            lengths = [got_ref[0, r].astype(jnp.int32) for r in range(responses)]
            advantages = [got_ref[0, responses + r] for r in range(responses)]
        ends = [sum(lengths[:r + 1]) for r in range(responses)]
        for copy in own_loads if part == 0 else got_loads:
            copy.wait()
        tok_seg = segment(lax.broadcasted_iota(jnp.int32, (tokens, HEAD), 0), ends)
        weight = jnp.zeros((tokens, HEAD), jnp.float32)
        for r in range(responses):
            weight = jnp.where(tok_seg == r, advantages[r], weight)
        for g in range(GROUP):
            cols = head_cols(g, HALF)
            do = weight * tok_ref[part, :, cols].astype(jnp.float32)
            tok_ref[part, :, cols] = do.astype(jnp.bfloat16)
        for g in range(GROUP):
            qt_ref[:, tok_cols(g)] = turn(tok_ref[part, :, head_cols(g)])
            dot_t_ref[:, tok_cols(g)] = turn(tok_ref[part, :, head_cols(g, HALF)])

        u = lax.broadcasted_iota(jnp.int32, (tokens, tokens), 0)
        t = lax.broadcasted_iota(jnp.int32, (tokens, tokens), 1)
        near = (segment(u, ends) == segment(t, ends)) & (u <= t)
        near_keys = tok_ref[part, :, K_COLS]
        kt_ref[:, prompt:] = turn(near_keys)
        forward(near_keys, tok_ref[part, :, V_COLS], prompt, near)
        for c in range(chunks):
            at = slice(c * CHUNK, (c + 1) * CHUNK)
            if part == 0:
                kv_loads[c].wait()
                kt_ref[:, at] = turn(kv_ref[at, :HEAD])
            forward(kv_ref[at, :HEAD], kv_ref[at, HEAD:], c * CHUNK, None)

        deltas = []
        for g in range(GROUP):
            peak = peak_ref[:, tok_cols(g)]
            top = jnp.max(peak, axis=0, keepdims=True)
            share = jnp.exp2((peak - top) * scale)
            row_sum = jnp.sum(share * sum_ref[:, tok_cols(g)], axis=0, keepdims=True)
            weighted = jnp.sum(share * dot_ref[:, tok_cols(g)], axis=0, keepdims=True)
            inverse = 1.0 / row_sum
            peak_ref[:, tok_cols(g)] = share * inverse
            deltas.append(jnp.broadcast_to(weighted * inverse, (8, tokens)))

        for c in range(chunks):
            at = slice(c * CHUNK, (c + 1) * CHUNK)
            key_grad, value_grad = backward(part, c * CHUNK, CHUNK, deltas)
            if part == 0:
                sum_kv_ref[at, :HEAD], sum_kv_ref[at, HEAD:] = key_grad, value_grad
            if part == parts - 1:
                gkv_ref[at, :HEAD] = (sum_kv_ref[at, :HEAD] + key_grad).astype(jnp.bfloat16)
                gkv_ref[at, HEAD:] = (sum_kv_ref[at, HEAD:] + value_grad).astype(jnp.bfloat16)
                store(gkv_ref.at[pl.ds(c * CHUNK, CHUNK)], gkv_hbm.at[pl.ds(c * CHUNK, CHUNK)])
        key_grad, value_grad = backward(part, prompt, tokens, deltas)
        grad_ref[part, :, GK_COLS] = key_grad.astype(jnp.bfloat16)
        grad_ref[part, :, GV_COLS] = value_grad.astype(jnp.bfloat16)
        for g in range(GROUP):
            grad_ref[part, :, head_cols(g)] = (gqt_ref[:, tok_cols(g)].T * factor).astype(jnp.bfloat16)
        if part == 0:
            store(grad_ref.at[0, :, Q_COLS], gq_hbm.at[:, query_cols])
            store(grad_ref.at[0, :, GK_COLS], gnk_hbm.at[:, own_cols])
            store(grad_ref.at[0, :, GV_COLS], gnv_hbm.at[:, own_cols])
        else:
            store(grad_ref.at[1], back_hbm)
    for copy in stores:
        copy.wait()


def attention(query, near_key, near_value, got_a, got_b, got, kv, out_grad, lengths, advantage):
    tokens = query.shape[0]
    prompt = kv.shape[0]
    span = prompt + tokens
    wide = GROUP * tokens
    back = (GROUP + 2) * HEAD
    smem = pl.BlockSpec(memory_space=pltpu.SMEM)
    here = pl.BlockSpec(memory_space=pl.ANY)
    bf16, f32 = jnp.bfloat16, jnp.float32
    return pl.pallas_call(
        attention_kernel,
        in_specs=[smem] * 3 + [here] * 7,
        out_specs=[here] * 5,
        out_shape=[
            jax.ShapeDtypeStruct(query.shape, bf16),
            jax.ShapeDtypeStruct(near_key.shape, bf16),
            jax.ShapeDtypeStruct(near_key.shape, bf16),
            jax.ShapeDtypeStruct((tokens, back), bf16),
            jax.ShapeDtypeStruct(kv.shape, bf16),
        ],
        scratch_shapes=[
            pltpu.VMEM((2, tokens, 2 * HALF), bf16),
            pltpu.VMEM((prompt, 2 * HEAD), bf16),
            pltpu.VMEM((2, tokens, back), bf16),
            pltpu.VMEM((prompt, 2 * HEAD), bf16),
            pltpu.VMEM((prompt, 2 * HEAD), f32),
            pltpu.VMEM((span, wide), f32),
            pltpu.VMEM((span, wide), f32),
            pltpu.VMEM((HEAD, span), bf16),
            pltpu.VMEM((HEAD, wide), bf16),
            pltpu.VMEM((HEAD, wide), bf16),
            pltpu.VMEM((HEAD, wide), f32),
            pltpu.VMEM((span // FOLD, wide), f32),
            pltpu.VMEM((span // FOLD, wide), f32),
            pltpu.VMEM((span // FOLD, wide), f32),
            pltpu.SemaphoreType.DMA((6,)),
            pltpu.SemaphoreType.DMA((prompt // CHUNK,)),
            pltpu.SemaphoreType.DMA((prompt // CHUNK + 4,)),
        ],
        compiler_params=pltpu.CompilerParams(vmem_limit_bytes=VMEM_MIB * 1024 * 1024),
        cost_estimate=pl.CostEstimate(
            flops=2 * 6 * 2 * GROUP * tokens * span * HEAD,
            bytes_accessed=8 * 1024 * 1024,
            transcendentals=2 * GROUP * tokens * span,
        ),
        name="attention",
    )(lengths, advantage, got, query, out_grad, near_key, near_value, got_a, got_b, kv)


NEAR = ("zh", "zl", "kvh")
FAR = ("x", "y")
SWAP = [(0, 1), (1, 0)]


def exchange(a, axes):
    return lax.all_to_all(a, axes, split_axis=0, concat_axis=0, tiled=True)


def pack_kernel(
    copies, len_ref, adv_ref, q_hbm, og_hbm, nk_hbm, nv_hbm, key_ref, value_ref,
    send_a_ref, send_b_ref, send_ref, first_ref, sem,
):
    other = 1 - lax.axis_index("zl")
    query_cols = pl.ds(pl.multiple_of(other * (GROUP * HEAD), HEAD), GROUP * HEAD)
    key_cols = pl.ds(pl.multiple_of(other * HEAD, HEAD), HEAD)
    moves = []
    for i, (source, cols, target, at) in enumerate([
        (q_hbm, query_cols, send_a_ref, pl.ds(0, GROUP * HEAD)),
        (nk_hbm, key_cols, send_a_ref, pl.ds(GROUP * HEAD, HEAD)),
        (og_hbm, query_cols, send_b_ref, pl.ds(0, GROUP * HEAD)),
        (nv_hbm, key_cols, send_b_ref, pl.ds(GROUP * HEAD, HEAD)),
    ]):
        moves.append(pltpu.make_async_copy(source.at[:, cols], target.at[:, at], sem.at[i]))
        moves[-1].start()
    responses = len_ref.shape[1]
    for r in range(responses):
        send_ref[0, r] = len_ref[0, r].astype(jnp.float32)
        send_ref[0, responses + r] = adv_ref[0, r]
    zl = 2
    kvh = KEY_VALUE_HEADS // zl
    rows = []
    for half in range(zl):
        for owner in range(kvh):
            cols = slice((owner * zl + half) * HEAD, (owner * zl + half + 1) * HEAD)
            rows.append(jnp.concatenate(
                [key_ref[:, cols].astype(jnp.float32), value_ref[:, cols].astype(jnp.float32)], axis=1
            ))
    rows = jnp.concatenate(rows, axis=0)
    count = rows.shape[0]
    rows = rows.astype(jnp.bfloat16)
    for c in range(copies):
        first_ref[c * count:(c + 1) * count, :] = rows
    for copy in moves:
        copy.wait()


def pack(copies, lengths, advantage, query, out_grad, near_key, near_value, key, value):
    tokens = query.shape[0]
    responses = lengths.shape[1]
    own = key.shape[0]
    smem = pl.BlockSpec(memory_space=pltpu.SMEM)
    vmem = pl.BlockSpec(memory_space=pltpu.VMEM)
    here = pl.BlockSpec(memory_space=pl.ANY)
    return pl.pallas_call(
        functools.partial(pack_kernel, copies),
        in_specs=[smem, smem] + [here] * 4 + [vmem] * 2,
        out_specs=[vmem, vmem, smem, vmem],
        out_shape=[
            jax.ShapeDtypeStruct((tokens, HALF), jnp.bfloat16),
            jax.ShapeDtypeStruct((tokens, HALF), jnp.bfloat16),
            jax.ShapeDtypeStruct((1, 2 * responses), jnp.float32),
            jax.ShapeDtypeStruct((copies * KEY_VALUE_HEADS * own, 2 * HEAD), jnp.bfloat16),
        ],
        scratch_shapes=[pltpu.SemaphoreType.DMA((4,))],
        name="pack",
    )(lengths, advantage, query, out_grad, near_key, near_value, key, value)


def finish(copies, part):
    rows = jnp.sum(part.astype(jnp.float32).reshape(copies, -1, 2 * HEAD), axis=0)
    zl = 2
    kvh = KEY_VALUE_HEADS // zl
    own = rows.shape[0] // KEY_VALUE_HEADS
    blocks = [
        rows[(half * kvh + owner) * own:(half * kvh + owner + 1) * own]
        for owner in range(kvh) for half in range(zl)
    ]
    return (
        jnp.concatenate([block[:, :HEAD] for block in blocks], axis=1),
        jnp.concatenate([block[:, HEAD:] for block in blocks], axis=1),
    )


def on_device(
    shape, query, response_keys, response_values, prompt_key, prompt_values, out_grad, lengths,
    advantage
):
    x, y, zh, zl, kvh = shape
    send_a, send_b, send, first = pack(
        zh, lengths, advantage, query, out_grad, response_keys, response_values, prompt_key,
        prompt_values
    )
    got_a = lax.ppermute(send_a, "zl", SWAP)
    got_b = lax.ppermute(send_b, "zl", SWAP)
    got = lax.ppermute(send, "zl", SWAP)

    block = exchange(first, NEAR)
    if TIE:
        block, got_a = lax.optimization_barrier((block, got_a))
    kv = exchange(jnp.broadcast_to(block[None], (x * y, *block.shape)).reshape(-1, 2 * HEAD), FAR)

    grad_query, grad_resp_key, grad_resp_value, back, grad_kv = attention(
        query, response_keys, response_values, got_a, got_b, got, kv, out_grad, lengths, advantage
    )

    back = lax.ppermute(back, "zl", SWAP)
    part = exchange(grad_kv, FAR).reshape(x * y, *block.shape)
    part = jnp.sum(part.astype(jnp.float32), axis=0).astype(jnp.bfloat16)
    grad_prompt_key, grad_prompt_value = finish(zh, exchange(part, NEAR))

    other = 1 - lax.axis_index("zl")
    grad_query = lax.dynamic_update_slice(grad_query, back[:, Q_COLS], (0, other * GROUP * HEAD))
    grad_resp_key = lax.dynamic_update_slice(grad_resp_key, back[:, GK_COLS], (0, other * HEAD))
    grad_resp_value = lax.dynamic_update_slice(grad_resp_value, back[:, GV_COLS], (0, other * HEAD))
    return (grad_query, grad_resp_key, grad_resp_value, grad_prompt_key, grad_prompt_value)


def solution(mesh):
    shape = (4, 2, 4, 2, 4)
    names = ("x", "y", "zh", "zl", "kvh")
    fine = Mesh(mesh.devices.reshape(shape), names)
    resp = names[:4]
    return jax.shard_map(
        functools.partial(on_device, shape),
        mesh=fine,
        in_specs=(
            P(resp, "kvh"),
            P(resp, "kvh"),
            P(resp, "kvh"),
            P(names, None),
            P(names, None),
            P(resp, "kvh"),
            P(resp, None),
            P(resp, None),
        ),
        out_specs=(
            P(resp, "kvh"),
            P(resp, "kvh"),
            P(resp, "kvh"),
            P(names, None),
            P(names, None),
        ),
        check_vma=False,
    )
```

time: 131 us -> 108 us (0.82)
  blocking collectives: 60.5 us -> 22.1 us
  waiting for transfers between devices: 12.3 us -> 38.1 us
  Pallas kernels: 35.1 us -> 23.2 us
  starting transfers between devices: 16 us -> 18 us
    all_to_all x3 -> x1, blocking collectives: 60.5 us -> 22.1 us  [exchange(): return lax.all_to_all(a, axes, split_axis=0, concat_axis=0, tiled=True)]
    all_to_all x3, waiting for transfers between devices: 12.3 us -> 29.4 us  [exchange(): return lax.all_to_all(a, axes, split_axis=0, concat_axis=0, tiled=True)]
    pallas_call x2, Pallas kernels: 35.1 us -> 23.2 us  [the longest x1 20.4 us: attention(): pl.pallas_call(attention_kernel, in_specs=[smem] * 3 + [here] * 7, out_sp...]
    ppermute x0 -> x4, waiting for transfers between devices: none -> 8.7 us  [the longest x1 8.7 us: on_device(): got = lax.ppermute(send, 'zl', SWAP)]
    ppermute x0 -> x4, starting transfers between devices: none -> 4.02 us  [the longest x1 2.55 us: on_device(): got_a = lax.ppermute(send_a, 'zl', SWAP)]
    all_to_all x3, starting transfers between devices: 16 us -> 13.9 us  [exchange(): return lax.all_to_all(a, axes, split_axis=0, concat_axis=0, tiled=True)]
    unnamed x16 -> x43, local copies, waits for them, and re-layouts: 1.55 us -> 3.21 us
  transfers between devices with their start and end apart: 3 -> 7, of which waited for: 1 -> 4; matrix products, arithmetic and copies ran while one was open for 1% -> 1% of each run, Pallas kernels for 27% -> 0%
where the time goes in v3:
time: 108 us; the launch traced here: 107 us
  waiting for transfers between devices  38.1 us (35%)
  Pallas kernels  23.2 us (21%)
  blocking collectives  22.1 us (20%)
  starting transfers between devices  18 us (17%)
  local copies, waits for them, and re-layouts  4.35 us (4%)
    all_to_all x3, waiting for transfers between devices, exchange(): return lax.all_to_all(a, axes, split_axis=0, concat_axis=0, tiled=True)  29.4 us
    all_to_all x1, blocking collectives, exchange(): return lax.all_to_all(a, axes, split_axis=0, concat_axis=0, tiled=True)  22.1 us
    pallas_call x1, Pallas kernels, attention(): pl.pallas_call(attention_kernel, in_specs=[smem] * 3 + [here] * 7, out_sp...  20.4 us
    all_to_all x3, starting transfers between devices, exchange(): return lax.all_to_all(a, axes, split_axis=0, concat_axis=0, tiled=True)  13.9 us
    ppermute x1, waiting for transfers between devices, on_device(): got = lax.ppermute(send, 'zl', SWAP)  8.7 us
    unnamed x43, local copies, waits for them, and re-layouts  3.21 us
    pallas_call x1, Pallas kernels, pack(): pl.pallas_call(functools.partial(pack_kernel, copies), in_specs=[smem, sm...  2.82 us
    ppermute x1, starting transfers between devices, on_device(): got_a = lax.ppermute(send_a, 'zl', SWAP)  2.55 us
  transfers between devices with their start and end apart: 7, of which 4 were waited for; matrix products, arithmetic and copies ran while one was open for 1% of the time, Pallas kernels for 0%

profile of v3, /device:TPU:1, one launch (start us, length us, event | category | flops | bytes accessed | tf_op | source)
XLA Modules:
  0.0 107.5 jit_solution(3685878820820558384)
XLA Ops:
  0.6 2.8 %pack.1 = (bf16[256,768]{1,0:T(8,128)(2,1)}, bf16[256,768]{1,0:T(8,128)(2,1)}, f32[1,4]{1,0:T(1,128)}, bf16[256,256]{1,0:T(8,128)(2,1)}) custom-call(s32[1,2]{1,0:T(1,128)} %len_ref.3, f32[1,2]{1,0:T(1,128)} %adv_ref.3, bf16[256,1280]{1,0:T(8,128)(2,1)} %q_hbm.3, bf16[256,1280]{1,0:T(8,128)(2,1)} %og_hbm.3, bf16[256,256]{1,0:T(8,128)(2,1)} %nk_hbm.3, ...), custom_call_target="tpu_custom_call" | custom-call | tf_op jit(solution)/shard_map/pack/pallas_call | solution.py:312
  3.5 2.6 %collective-permute-start.1 = (bf16[256,768]{1,0:T(8,128)(2,1)}, bf16[256,768]{1,0:T(8,128)(2,1)S(1)}, u32[]{:S(2)}, u32[]{:S(2)}) collective-permute-start(bf16[256,768]{1,0:T(8,128)(2,1)} %get-tuple-element.18), channel_id=1, source_target_pairs={{0,4},{4,0},{1,5},{5,1},{2,6},{6,2},{3,7},{7,3},{8,12},{12,8},{9,1... | collective-permute-start | bytes 1179656 | tf_op jit(solution)/shard_map/ppermute | solution.py:351
  6.0 22.1 %all_to_all.38 = bf16[32,8,256]{2,1,0:T(8,128)(2,1)S(1)} all-to-all(bf16[32,8,256]{2,1,0:T(8,128)(2,1)} %bitcast.12), channel_id=1, replica_groups=mesh['x'=4,'y'=2,'zh'=4,'zl'=2,'kvh'=4] {'zh','zl','kvh'}, dimensions={0} | all-to-all | bytes 262144 | tf_op jit(solution)/shard_map/all_to_all | solution.py:264
  28.1 1.0 broadcast_in_dim.2
  29.2 4.3 %all-to-all-start.1 = ((bf16[8,256,256]{2,1,0:T(8,128)(2,1)}), bf16[8,256,256]{2,1,0:T(8,128)(2,1)S(1)}, u32[]{:S(2)}, u32[]{:S(2)}) async-start(bf16[8,256,256]{2,1,0:T(8,128)(2,1)} %broadcast_in_dim.2), calls=%async_computation.1 | async-start | bytes 2097152 | tf_op jit(solution)/shard_map/all_to_all | solution.py:264
  33.5 0.5 collective-permute-start.2
  33.9 0.2 copy-done.17
  34.1 0.9 collective-permute-start
  35.0 8.7 %collective-permute-done.got_ref = f32[1,4]{1,0:T(1,128)S(1)} collective-permute-done((f32[1,4]{1,0:T(1,128)S(1)}, f32[1,4]{1,0:T(1,128)S(1)}, u32[]{:S(2)}, u32[]{:S(2)}) %collective-permute-start) | collective-permute-done | bytes 48 | tf_op jit(solution)/shard_map/ppermute | solution.py:353
  43.7 0.7 copy-done.6
  44.5 4.9 %all-to-all-done.1 = bf16[8,256,256]{2,1,0:T(8,128)(2,1)S(1)} async-done(((bf16[8,256,256]{2,1,0:T(8,128)(2,1)}), bf16[8,256,256]{2,1,0:T(8,128)(2,1)S(1)}, u32[]{:S(2)}, u32[]{:S(2)}) %all-to-all-start.1) | async-done | bytes 1048608 | tf_op jit(solution)/shard_map/all_to_all | solution.py:264
  49.4 1.0 copy-done.7
  50.4 20.4 %attention.1 = (bf16[256,1280]{1,0:T(8,128)(2,1)}, bf16[256,256]{1,0:T(8,128)(2,1)}, bf16[256,256]{1,0:T(8,128)(2,1)}, bf16[256,896]{1,0:T(8,128)(2,1)S(1)}, bf16[2048,256]{1,0:T(8,128)(2,1)}) custom-call(s32[1,2]{1,0:T(1,128)S(1)} %copy-done.4, f32[1,2]{1,0:T(1,128)S(1)} %copy-done.5, f32[1,4]{1,0:T(1,128)S(1)} %collective-permute-done.got_ref, ...), custom_call_target="tpu_custom_call" | custom-call | flops 9059696640 | bytes 8388608 | tf_op jit(solution)/shard_map/attention/pallas_call | solution.py:218
  70.8 3.6 %all-to-all-start.2 = ((bf16[8,256,256]{2,1,0:T(8,128)(2,1)}), bf16[8,256,256]{2,1,0:T(8,128)(2,1)S(1)}, u32[]{:S(2)}, u32[]{:S(2)}) async-start(bf16[8,256,256]{2,1,0:T(8,128)(2,1)} %bitcast.3), calls=%async_computation.2 | async-start | bytes 2097152 | tf_op jit(solution)/shard_map/all_to_all | solution.py:264
  74.4 0.1 collective-permute-start.3
  74.5 14.5 %all-to-all-done.2 = bf16[8,256,256]{2,1,0:T(8,128)(2,1)S(1)} async-done(((bf16[8,256,256]{2,1,0:T(8,128)(2,1)}), bf16[8,256,256]{2,1,0:T(8,128)(2,1)S(1)}, u32[]{:S(2)}, u32[]{:S(2)}) %all-to-all-start.2) | async-done | bytes 1048608 | tf_op jit(solution)/shard_map/all_to_all | solution.py:264
  89.0 0.8 reduce_sum.21
  89.8 6.1 %all-to-all-start.3 = ((bf16[32,8,256]{2,1,0:T(8,128)(2,1)}), bf16[32,8,256]{2,1,0:T(8,128)(2,1)S(1)}, u32[]{:S(2)}, u32[]{:S(2)}) async-start(bf16[32,8,256]{2,1,0:T(8,128)(2,1)} %bitcast.4), calls=%async_computation.3 | async-start | bytes 262144 | tf_op jit(solution)/shard_map/all_to_all | solution.py:264
  96.1 0.6 copy-done.14
  96.7 0.0 copy-done.16
  96.7 10.0 %all-to-all-done.3 = bf16[32,8,256]{2,1,0:T(8,128)(2,1)S(1)} async-done(((bf16[32,8,256]{2,1,0:T(8,128)(2,1)}), bf16[32,8,256]{2,1,0:T(8,128)(2,1)S(1)}, u32[]{:S(2)}, u32[]{:S(2)}) %all-to-all-start.3) | async-done | bytes 131104 | tf_op jit(solution)/shard_map/all_to_all | solution.py:264
  106.8 0.0 copy-start.9
  106.9 0.6 copy-done.8
  107.4 0.0 copy-done.9
  (42 shorter events, 0.2 us)
Async XLA Ops:
  3.5 24.6 %collective-permute-start.1 = (bf16[256,768]{1,0:T(8,128)(2,1)}, bf16[256,768]{1,0:T(8,128)(2,1)S(1)}, u32[]{:S(2)}, u32[]{:S(2)}) collective-permute-start(bf16[256,768]{1,0:T(8,128)(2,1)} %get-tuple-element.18), channel_id=1, source_target_pairs={{0,4},{4,0},{1,5},{5,1},{2,6},{6,2},{3,7},{7,3},{8,12},{12,8},{9,1... | collective-permute-start | bytes 1179656 | tf_op jit(solution)/shard_map/ppermute | solution.py:351
  29.1 4.3 %copy-start.12 = (bf16[256,768]{1,0:T(8,128)(2,1)S(1)}, bf16[256,768]{1,0:T(8,128)(2,1)}, u32[]{:S(2)}) copy-start(bf16[256,768]{1,0:T(8,128)(2,1)} %get-tuple-element.20) | copy-start | bytes 1179652
  29.1 20.3 %copy-start = (bf16[256,1280]{1,0:T(8,128)(2,1)S(1)}, bf16[256,1280]{1,0:T(8,128)(2,1)}, u32[]{:S(2)}) copy-start(bf16[256,1280]{1,0:T(8,128)(2,1)} %q_hbm.3) | copy-start | bytes 1966084
  29.1 20.3 %copy-start.1 = (bf16[256,1280]{1,0:T(8,128)(2,1)S(1)}, bf16[256,1280]{1,0:T(8,128)(2,1)}, u32[]{:S(2)}) copy-start(bf16[256,1280]{1,0:T(8,128)(2,1)} %og_hbm.3) | copy-start | bytes 1966084
  29.1 20.3 %copy-start.2 = (bf16[256,256]{1,0:T(8,128)(2,1)S(1)}, bf16[256,256]{1,0:T(8,128)(2,1)}, u32[]{:S(2)}) copy-start(bf16[256,256]{1,0:T(8,128)(2,1)} %nk_hbm.3) | copy-start | bytes 393220
  29.1 20.3 %copy-start.3 = (bf16[256,256]{1,0:T(8,128)(2,1)S(1)}, bf16[256,256]{1,0:T(8,128)(2,1)}, u32[]{:S(2)}) copy-start(bf16[256,256]{1,0:T(8,128)(2,1)} %nv_hbm.3) | copy-start | bytes 393220
  29.2 20.2 %all-to-all-start.1 = ((bf16[8,256,256]{2,1,0:T(8,128)(2,1)}), bf16[8,256,256]{2,1,0:T(8,128)(2,1)S(1)}, u32[]{:S(2)}, u32[]{:S(2)}) async-start(bf16[8,256,256]{2,1,0:T(8,128)(2,1)} %broadcast_in_dim.2), calls=%async_computation.1 | async-start | bytes 2097152 | tf_op jit(solution)/shard_map/all_to_all | solution.py:264
  33.4 0.7 copy-start.17
  33.5 10.3 %collective-permute-start.2 = (bf16[256,768]{1,0:T(8,128)(2,1)S(1)}, bf16[256,768]{1,0:T(8,128)(2,1)S(1)}, u32[]{:S(2)}, u32[]{:S(2)}) collective-permute-start(bf16[256,768]{1,0:T(8,128)(2,1)S(1)} %copy-done.12), channel_id=1, source_target_pairs={{0,4},{4,0},{1,5},{5,1},{2,6},{6,2},{3,7},{7,3},{8,12},{12,8},{9,1... | collective-permute-start | bytes 1179656 | tf_op jit(solution)/shard_map/ppermute | solution.py:352
  34.1 15.3 %copy-start.4 = (s32[1,2]{1,0:T(1,128)S(1)}, s32[1,2]{1,0:T(1,128)}, u32[]{:S(2)}) copy-start(s32[1,2]{1,0:T(1,128)} %len_ref.3) | copy-start | bytes 28
  34.1 15.3 %copy-start.5 = (f32[1,2]{1,0:T(1,128)S(1)}, f32[1,2]{1,0:T(1,128)}, u32[]{:S(2)}) copy-start(f32[1,2]{1,0:T(1,128)} %adv_ref.3) | copy-start | bytes 28
  34.1 9.6 %collective-permute-start = (f32[1,4]{1,0:T(1,128)S(1)}, f32[1,4]{1,0:T(1,128)S(1)}, u32[]{:S(2)}, u32[]{:S(2)}) collective-permute-start(f32[1,4]{1,0:T(1,128)S(1)} %copy-done.17), channel_id=1, source_target_pairs={{0,4},{4,0},{1,5},{5,1},{2,6},{6,2},{3,7},{7,3},{8,12},{12,8},{9,1... | collective-permute-start | bytes 56 | tf_op jit(solution)/shard_map/ppermute | solution.py:353
  43.7 0.7 copy-start.6
  49.4 1.0 copy-start.7
  70.8 18.2 %all-to-all-start.2 = ((bf16[8,256,256]{2,1,0:T(8,128)(2,1)}), bf16[8,256,256]{2,1,0:T(8,128)(2,1)S(1)}, u32[]{:S(2)}, u32[]{:S(2)}) async-start(bf16[8,256,256]{2,1,0:T(8,128)(2,1)} %bitcast.3), calls=%async_computation.2 | async-start | bytes 2097152 | tf_op jit(solution)/shard_map/all_to_all | solution.py:264
  74.4 21.6 %collective-permute-start.3 = (bf16[256,896]{1,0:T(8,128)(2,1)S(1)}, bf16[256,896]{1,0:T(8,128)(2,1)S(1)}, u32[]{:S(2)}, u32[]{:S(2)}) collective-permute-start(bf16[256,896]{1,0:T(8,128)(2,1)S(1)} %get-tuple-element.23), channel_id=1, source_target_pairs={{0,4},{4,0},{1,5},{5,1},{2,6},{6,2},{3,7},{7,3},{8,12},{12,8},{9,1... | collective-permute-start | bytes 1376264 | tf_op jit(solution)/shard_map/ppermute | solution.py:364
  74.5 21.5 %copy-start.10 = (bf16[256,1280]{1,0:T(8,128)(2,1)S(1)}, bf16[256,1280]{1,0:T(8,128)(2,1)}, u32[]{:S(2)}) copy-start(bf16[256,1280]{1,0:T(8,128)(2,1)} %get-tuple-element.22) | copy-start | bytes 1966084
  89.8 6.1 %copy-start.13 = (bf16[256,256]{1,0:T(8,128)(2,1)S(1)}, bf16[256,256]{1,0:T(8,128)(2,1)}, u32[]{:S(2)}) copy-start(bf16[256,256]{1,0:T(8,128)(2,1)} %get-tuple-element.24) | copy-start | bytes 393220
  89.8 6.1 %copy-start.15 = (bf16[256,256]{1,0:T(8,128)(2,1)S(1)}, bf16[256,256]{1,0:T(8,128)(2,1)}, u32[]{:S(2)}) copy-start(bf16[256,256]{1,0:T(8,128)(2,1)} %get-tuple-element.25) | copy-start | bytes 393220
  89.8 16.9 %all-to-all-start.3 = ((bf16[32,8,256]{2,1,0:T(8,128)(2,1)}), bf16[32,8,256]{2,1,0:T(8,128)(2,1)S(1)}, u32[]{:S(2)}, u32[]{:S(2)}) async-start(bf16[32,8,256]{2,1,0:T(8,128)(2,1)} %bitcast.4), calls=%async_computation.3 | async-start | bytes 262144 | tf_op jit(solution)/shard_map/all_to_all | solution.py:264
  96.0 0.7 copy-start.14
  96.0 0.7 copy-start.16
  96.7 10.1 %copy-start.11 = (bf16[256,1280]{1,0:T(8,128)(2,1)}, bf16[256,1280]{1,0:T(8,128)(2,1)S(1)}, u32[]{:S(2)}) copy-start(bf16[256,1280]{1,0:T(8,128)(2,1)S(1)} %slice_dynamic-update-slice_fusion) | copy-start | bytes 1966084
  106.8 0.6 copy-start.9
  (1 other events, 0.6 us)

commit v4 on v3

v4 whole, which is shorter than its diff:
```python
import functools
import math

import jax
import jax.numpy as jnp
from jax import lax
from jax.experimental import pallas as pl
from jax.experimental.pallas import tpu as pltpu
from jax.sharding import Mesh
from jax.sharding import PartitionSpec as P

QUERY_HEADS = 40
KEY_VALUE_HEADS = 8
HEAD = 128
GROUP = QUERY_HEADS // KEY_VALUE_HEADS
CHUNK = 512
FOLD = 16
PROMPT_TOKENS = 2048
VMEM_MIB = 38
TIE = True
HALF = (GROUP + 1) * HEAD
Q_COLS = slice(0, GROUP * HEAD)
K_COLS = slice(GROUP * HEAD, HALF)
O_COLS = slice(HALF, HALF + GROUP * HEAD)
V_COLS = slice(HALF + GROUP * HEAD, 2 * HALF)
GK_COLS = slice(GROUP * HEAD, (GROUP + 1) * HEAD)
GV_COLS = slice((GROUP + 1) * HEAD, (GROUP + 2) * HEAD)
LOG2E = 1.4426950408889634

NN = (((1,), (0,)), ((), ()))


def dot(a, b, dims):
    return lax.dot_general(a, b, dims, preferred_element_type=jnp.float32)


def attention_kernel(part, *refs):
    if part == 0:
        len_ref, adv_ref, q_hbm, og_hbm, nk_hbm, nv_hbm, kv_hbm = refs[:7]
        gq_hbm, gnk_hbm, gnv_hbm, sum_hbm = refs[7:11]
    else:
        got_ref, got_hbm, kv_hbm, sum_hbm, back_hbm, gkv_hbm = refs[:6]
    (tok_ref, kv_ref, grad_ref, gkv_ref, sum_kv_ref,
     p_ref, d_ref, kt_ref, qt_ref, dot_t_ref, gqt_ref,
     peak_ref, sum_ref, dot_ref, in_sem, kv_sem, out_sem) = refs[-17:]
    tokens = tok_ref.shape[0]
    prompt = kv_ref.shape[0]
    chunks = prompt // CHUNK
    factor = 1.0 / math.sqrt(HEAD)
    scale = factor * LOG2E

    if part == 0:
        mine = lax.axis_index("zl")
        query_cols = pl.ds(pl.multiple_of(mine * (GROUP * HEAD), HEAD), GROUP * HEAD)
        own_cols = pl.ds(pl.multiple_of(mine * HEAD, HEAD), HEAD)
        loads = [
            pltpu.make_async_copy(q_hbm.at[:, query_cols], tok_ref.at[:, Q_COLS], in_sem.at[0]),
            pltpu.make_async_copy(og_hbm.at[:, query_cols], tok_ref.at[:, O_COLS], in_sem.at[1]),
            pltpu.make_async_copy(nk_hbm.at[:, own_cols], tok_ref.at[:, K_COLS], in_sem.at[2]),
            pltpu.make_async_copy(nv_hbm.at[:, own_cols], tok_ref.at[:, V_COLS], in_sem.at[3]),
        ]
    else:
        loads = [pltpu.make_async_copy(got_hbm, tok_ref, in_sem.at[0])]
    for copy in loads:
        copy.start()
    kv_loads, sum_loads = [], []
    for c in range(chunks):
        at = pl.ds(c * CHUNK, CHUNK)
        kv_loads.append(pltpu.make_async_copy(kv_hbm.at[at], kv_ref.at[at], kv_sem.at[c]))
        kv_loads[-1].start()
    if part == 1:
        sum_loads.append(pltpu.make_async_copy(sum_hbm, sum_kv_ref, in_sem.at[1]))
        sum_loads[-1].start()

    def segment(pos, ends):
        seg = jnp.zeros(pos.shape, jnp.int32)
        for end in ends:
            seg = seg + (pos >= end).astype(jnp.int32)
        return seg

    def head_cols(g, first=0):
        return slice(first + g * HEAD, first + (g + 1) * HEAD)

    def tok_cols(g):
        return slice(g * tokens, (g + 1) * tokens)

    def turn(a):
        return a.astype(jnp.float32).T.astype(jnp.bfloat16)

    def forward(keys, values, row, mask):
        size = keys.shape[0]
        groups = size // (8 * FOLD)
        for g in range(GROUP):
            s = dot(keys, qt_ref[:, tok_cols(g)], NN)
            if mask is not None:
                s = jnp.where(mask, s, -1e30)
            d = dot(values, dot_t_ref[:, tok_cols(g)], NN)
            s = s.reshape(groups, FOLD, 8, tokens)
            d_ref[row:row + size, tok_cols(g)] = d
            d = d.reshape(groups, FOLD, 8, tokens)
            for i in range(groups):
                slot = row // FOLD + 8 * i
                key = row + 8 * FOLD * i
                peak = jnp.max(s[i], axis=0)
                e = jnp.exp2((s[i] - peak[None]) * scale)
                p_ref[key:key + 8 * FOLD, tok_cols(g)] = e.reshape(8 * FOLD, tokens)
                peak_ref[slot:slot + 8, tok_cols(g)] = peak
                sum_ref[slot:slot + 8, tok_cols(g)] = jnp.sum(e, axis=0)
                dot_ref[slot:slot + 8, tok_cols(g)] = jnp.sum(e * d[i], axis=0)

    def backward(row, size, deltas):
        groups = size // (8 * FOLD)
        slot = row // FOLD
        key_sum = jnp.zeros((size, HEAD), jnp.float32)
        value_sum = jnp.zeros((size, HEAD), jnp.float32)
        for g in range(GROUP):
            p = p_ref[row:row + size, tok_cols(g)].reshape(groups, FOLD, 8, tokens)
            d = d_ref[row:row + size, tok_cols(g)].reshape(groups, FOLD, 8, tokens)
            share = peak_ref[slot:slot + 8 * groups, tok_cols(g)].reshape(groups, 1, 8, tokens)
            p = p * share
            ds = p * (d - deltas[g][None, None])
            p = p.reshape(size, tokens).astype(jnp.bfloat16)
            ds = ds.reshape(size, tokens).astype(jnp.bfloat16)
            key_sum = key_sum + dot(ds, tok_ref[:, head_cols(g)], NN)
            value_sum = value_sum + dot(p, tok_ref[:, head_cols(g, HALF)], NN)
            query_sum = dot(kt_ref[:, row:row + size], ds, NN)
            if row == kt_ref.shape[1] - tokens:
                gqt_ref[:, tok_cols(g)] = query_sum
            else:
                gqt_ref[:, tok_cols(g)] += query_sum
        return key_sum * factor, value_sum

    stores = []

    def store(source, target):
        stores.append(pltpu.make_async_copy(source, target, out_sem.at[len(stores)]))
        stores[-1].start()

    if part == 0:
        responses = len_ref.shape[1]
        lengths = [len_ref[0, r] for r in range(responses)]
        advantages = [adv_ref[0, r] for r in range(responses)]
    else:
        responses = got_ref.shape[1] // 2
        lengths = [got_ref[0, r].astype(jnp.int32) for r in range(responses)]
        advantages = [got_ref[0, responses + r] for r in range(responses)]
    ends = [sum(lengths[:r + 1]) for r in range(responses)]
    for copy in loads:
        copy.wait()
    tok_seg = segment(lax.broadcasted_iota(jnp.int32, (tokens, HEAD), 0), ends)
    weight = jnp.zeros((tokens, HEAD), jnp.float32)
    for r in range(responses):
        weight = jnp.where(tok_seg == r, advantages[r], weight)
    for g in range(GROUP):
        cols = head_cols(g, HALF)
        do = weight * tok_ref[:, cols].astype(jnp.float32)
        tok_ref[:, cols] = do.astype(jnp.bfloat16)
    for g in range(GROUP):
        qt_ref[:, tok_cols(g)] = turn(tok_ref[:, head_cols(g)])
        dot_t_ref[:, tok_cols(g)] = turn(tok_ref[:, head_cols(g, HALF)])

    u = lax.broadcasted_iota(jnp.int32, (tokens, tokens), 0)
    t = lax.broadcasted_iota(jnp.int32, (tokens, tokens), 1)
    near = (segment(u, ends) == segment(t, ends)) & (u <= t)
    near_keys = tok_ref[:, K_COLS]
    kt_ref[:, prompt:] = turn(near_keys)
    forward(near_keys, tok_ref[:, V_COLS], prompt, near)
    for c in range(chunks):
        at = slice(c * CHUNK, (c + 1) * CHUNK)
        kv_loads[c].wait()
        kt_ref[:, at] = turn(kv_ref[at, :HEAD])
        forward(kv_ref[at, :HEAD], kv_ref[at, HEAD:], c * CHUNK, None)

    deltas = []
    for g in range(GROUP):
        peak = peak_ref[:, tok_cols(g)]
        top = jnp.max(peak, axis=0, keepdims=True)
        share = jnp.exp2((peak - top) * scale)
        row_sum = jnp.sum(share * sum_ref[:, tok_cols(g)], axis=0, keepdims=True)
        weighted = jnp.sum(share * dot_ref[:, tok_cols(g)], axis=0, keepdims=True)
        inverse = 1.0 / row_sum
        peak_ref[:, tok_cols(g)] = share * inverse
        deltas.append(jnp.broadcast_to(weighted * inverse, (8, tokens)))

    for copy in sum_loads:
        copy.wait()
    key_grad, value_grad = backward(prompt, tokens, deltas)
    grad_ref[:, GK_COLS] = key_grad.astype(jnp.bfloat16)
    grad_ref[:, GV_COLS] = value_grad.astype(jnp.bfloat16)
    for c in range(chunks):
        at = slice(c * CHUNK, (c + 1) * CHUNK)
        block = pl.ds(c * CHUNK, CHUNK)
        key_grad, value_grad = backward(c * CHUNK, CHUNK, deltas)
        if part == 0:
            sum_kv_ref[at, :HEAD], sum_kv_ref[at, HEAD:] = key_grad, value_grad
            store(sum_kv_ref.at[block], sum_hbm.at[block])
        else:
            gkv_ref[at, :HEAD] = (sum_kv_ref[at, :HEAD] + key_grad).astype(jnp.bfloat16)
            gkv_ref[at, HEAD:] = (sum_kv_ref[at, HEAD:] + value_grad).astype(jnp.bfloat16)
            store(gkv_ref.at[block], gkv_hbm.at[block])
    for g in range(GROUP):
        grad_ref[:, head_cols(g)] = (gqt_ref[:, tok_cols(g)].T * factor).astype(jnp.bfloat16)
    if part == 0:
        store(grad_ref.at[:, Q_COLS], gq_hbm.at[:, query_cols])
        store(grad_ref.at[:, GK_COLS], gnk_hbm.at[:, own_cols])
        store(grad_ref.at[:, GV_COLS], gnv_hbm.at[:, own_cols])
    else:
        store(grad_ref, back_hbm)
    for copy in stores:
        copy.wait()


def attention(part, smem_args, args, out_shape):
    tokens = args[0].shape[0]
    prompt = PROMPT_TOKENS
    span = prompt + tokens
    wide = GROUP * tokens
    smem = pl.BlockSpec(memory_space=pltpu.SMEM)
    here = pl.BlockSpec(memory_space=pl.ANY)
    bf16, f32 = jnp.bfloat16, jnp.float32
    return pl.pallas_call(
        functools.partial(attention_kernel, part),
        in_specs=[smem] * len(smem_args) + [here] * len(args),
        out_specs=[here] * len(out_shape),
        out_shape=out_shape,
        scratch_shapes=[
            pltpu.VMEM((tokens, 2 * HALF), bf16),
            pltpu.VMEM((prompt, 2 * HEAD), bf16),
            pltpu.VMEM((tokens, (GROUP + 2) * HEAD), bf16),
            pltpu.VMEM((prompt, 2 * HEAD), bf16),
            pltpu.VMEM((prompt, 2 * HEAD), f32),
            pltpu.VMEM((span, wide), f32),
            pltpu.VMEM((span, wide), f32),
            pltpu.VMEM((HEAD, span), bf16),
            pltpu.VMEM((HEAD, wide), bf16),
            pltpu.VMEM((HEAD, wide), bf16),
            pltpu.VMEM((HEAD, wide), f32),
            pltpu.VMEM((span // FOLD, wide), f32),
            pltpu.VMEM((span // FOLD, wide), f32),
            pltpu.VMEM((span // FOLD, wide), f32),
            pltpu.SemaphoreType.DMA((4,)),
            pltpu.SemaphoreType.DMA((prompt // CHUNK,)),
            pltpu.SemaphoreType.DMA((prompt // CHUNK + 3,)),
        ],
        compiler_params=pltpu.CompilerParams(vmem_limit_bytes=VMEM_MIB * 1024 * 1024),
        cost_estimate=pl.CostEstimate(
            flops=2 * 6 * GROUP * tokens * span * HEAD,
            bytes_accessed=4 * 1024 * 1024,
            transcendentals=GROUP * tokens * span,
        ),
        name="attention",
    )(*smem_args, *args)


NEAR = ("zh", "zl", "kvh")
FAR = ("x", "y")
SWAP = [(0, 1), (1, 0)]


def exchange(a, axes):
    return lax.all_to_all(a, axes, split_axis=0, concat_axis=0, tiled=True)


def rows_kernel(copies, key_ref, value_ref, first_ref):
    zl = 2
    kvh = KEY_VALUE_HEADS // zl
    rows = []
    for half in range(zl):
        for owner in range(kvh):
            cols = slice((owner * zl + half) * HEAD, (owner * zl + half + 1) * HEAD)
            rows.append(jnp.concatenate(
                [key_ref[:, cols].astype(jnp.float32), value_ref[:, cols].astype(jnp.float32)], axis=1
            ))
    rows = jnp.concatenate(rows, axis=0)
    count = rows.shape[0]
    rows = rows.astype(jnp.bfloat16)
    for c in range(copies):
        first_ref[c * count:(c + 1) * count, :] = rows


def pack_kernel(len_ref, adv_ref, q_hbm, og_hbm, nk_hbm, nv_hbm, send_ref, scalars_ref, sem):
    other = 1 - lax.axis_index("zl")
    query_cols = pl.ds(pl.multiple_of(other * (GROUP * HEAD), HEAD), GROUP * HEAD)
    key_cols = pl.ds(pl.multiple_of(other * HEAD, HEAD), HEAD)
    moves = [
        pltpu.make_async_copy(q_hbm.at[:, query_cols], send_ref.at[:, Q_COLS], sem.at[0]),
        pltpu.make_async_copy(og_hbm.at[:, query_cols], send_ref.at[:, O_COLS], sem.at[1]),
        pltpu.make_async_copy(nk_hbm.at[:, key_cols], send_ref.at[:, K_COLS], sem.at[2]),
        pltpu.make_async_copy(nv_hbm.at[:, key_cols], send_ref.at[:, V_COLS], sem.at[3]),
    ]
    for move in moves:
        move.start()
    responses = len_ref.shape[1]
    for r in range(responses):
        scalars_ref[0, r] = len_ref[0, r].astype(jnp.float32)
        scalars_ref[0, responses + r] = adv_ref[0, r]
    for move in moves:
        move.wait()


def pack(lengths, advantage, query, out_grad, near_key, near_value):
    smem = pl.BlockSpec(memory_space=pltpu.SMEM)
    vmem = pl.BlockSpec(memory_space=pltpu.VMEM)
    here = pl.BlockSpec(memory_space=pl.ANY)
    return pl.pallas_call(
        pack_kernel,
        in_specs=[smem, smem] + [here] * 4,
        out_specs=[vmem, smem],
        out_shape=[
            jax.ShapeDtypeStruct((query.shape[0], 2 * HALF), jnp.bfloat16),
            jax.ShapeDtypeStruct((1, 2 * lengths.shape[1]), jnp.float32),
        ],
        scratch_shapes=[pltpu.SemaphoreType.DMA((4,))],
        name="pack",
    )(lengths, advantage, query, out_grad, near_key, near_value)


def finish(copies, part):
    rows = jnp.sum(part.astype(jnp.float32).reshape(copies, -1, 2 * HEAD), axis=0)
    zl = 2
    kvh = KEY_VALUE_HEADS // zl
    own = rows.shape[0] // KEY_VALUE_HEADS
    blocks = [
        rows[(half * kvh + owner) * own:(half * kvh + owner + 1) * own]
        for owner in range(kvh) for half in range(zl)
    ]
    return (
        jnp.concatenate([block[:, :HEAD] for block in blocks], axis=1),
        jnp.concatenate([block[:, HEAD:] for block in blocks], axis=1),
    )


def on_device(
    shape, query, response_keys, response_values, prompt_key, prompt_values, out_grad, lengths,
    advantage
):
    x, y, zh, zl, kvh = shape
    own = prompt_key.shape[0]
    first = pl.pallas_call(
        functools.partial(rows_kernel, zh),
        out_shape=jax.ShapeDtypeStruct((zh * KEY_VALUE_HEADS * own, 2 * HEAD), jnp.bfloat16),
        name="rows",
    )(prompt_key, prompt_values)
    block = exchange(first, NEAR)
    send, scalars = pack(lengths, advantage, query, out_grad, response_keys, response_values)
    if TIE:
        block, send, scalars = lax.optimization_barrier((block, send, scalars))
    got = lax.ppermute(send, "zl", SWAP)
    got_scalars = lax.ppermute(scalars, "zl", SWAP)
    kv = exchange(jnp.broadcast_to(block[None], (x * y, *block.shape)).reshape(-1, 2 * HEAD), FAR)

    def like(a, dtype=jnp.bfloat16):
        return jax.ShapeDtypeStruct(a.shape, dtype)

    grad_query, grad_resp_key, grad_resp_value, sums = attention(
        0, (lengths, advantage), (query, out_grad, response_keys, response_values, kv),
        [like(query), like(response_keys), like(response_values), like(kv, jnp.float32)],
    )
    back_shape = jax.ShapeDtypeStruct((query.shape[0], (GROUP + 2) * HEAD), jnp.bfloat16)
    back, grad_kv = attention(1, (got_scalars,), (got, kv, sums), [back_shape, like(kv)])

    back = lax.ppermute(back, "zl", SWAP)
    part = exchange(grad_kv, FAR).reshape(x * y, *block.shape)
    part = jnp.sum(part.astype(jnp.float32), axis=0).astype(jnp.bfloat16)
    grad_prompt_key, grad_prompt_value = finish(zh, exchange(part, NEAR))

    other = 1 - lax.axis_index("zl")
    grad_query = lax.dynamic_update_slice(grad_query, back[:, Q_COLS], (0, other * GROUP * HEAD))
    grad_resp_key = lax.dynamic_update_slice(grad_resp_key, back[:, GK_COLS], (0, other * HEAD))
    grad_resp_value = lax.dynamic_update_slice(grad_resp_value, back[:, GV_COLS], (0, other * HEAD))
    return (grad_query, grad_resp_key, grad_resp_value, grad_prompt_key, grad_prompt_value)


def solution(mesh):
    shape = (4, 2, 4, 2, 4)
    names = ("x", "y", "zh", "zl", "kvh")
    fine = Mesh(mesh.devices.reshape(shape), names)
    resp = names[:4]
    return jax.shard_map(
        functools.partial(on_device, shape),
        mesh=fine,
        in_specs=(
            P(resp, "kvh"),
            P(resp, "kvh"),
            P(resp, "kvh"),
            P(names, None),
            P(names, None),
            P(resp, "kvh"),
            P(resp, None),
            P(resp, None),
        ),
        out_specs=(
            P(resp, "kvh"),
            P(resp, "kvh"),
            P(resp, "kvh"),
            P(names, None),
            P(names, None),
        ),
        check_vma=False,
    )
```

time: 108 us -> 107 us (level)
  blocking collectives: 22.1 us -> 0 us
  starting transfers between devices: 18 us -> 28.1 us
  waiting for transfers between devices: 38.1 us -> 47.5 us
  Pallas kernels: 23.2 us -> 26.9 us
  local copies, waits for them, and re-layouts: 4.35 us -> 1.83 us
    all_to_all x1 -> x0, blocking collectives: 22.1 us -> none  [exchange(): return lax.all_to_all(a, axes, split_axis=0, concat_axis=0, tiled=True)]
    all_to_all x3 -> x4, waiting for transfers between devices: 29.4 us -> 47.4 us  [exchange(): return lax.all_to_all(a, axes, split_axis=0, concat_axis=0, tiled=True)]
    all_to_all x3 -> x4, starting transfers between devices: 13.9 us -> 26.5 us  [exchange(): return lax.all_to_all(a, axes, split_axis=0, concat_axis=0, tiled=True)]
    ppermute x1, waiting for transfers between devices: 8.7 us -> 0.01 us  [on_device(): got = lax.ppermute(send, 'zl', SWAP)]
    pallas_call x2 -> x4, Pallas kernels: 23.2 us -> 26.9 us  [the longest x2 22.6 us: attention(): pl.pallas_call(functools.partial(attention_kernel, part), in_specs=[smem]...]
    unnamed x43 -> x37, local copies, waits for them, and re-layouts: 3.21 us -> 0.69 us
    ppermute x2 -> x1, starting transfers between devices: 3.02 us -> 1.09 us  [on_device(): got_scalars = lax.ppermute(scalars, 'zl', SWAP)]
  transfers between devices with their start and end apart: 7 -> 7, of which waited for: 4 -> 4; matrix products, arithmetic and copies ran while one was open for 1% -> 1% of each run, Pallas kernels for 0% -> 14%
where the time goes in v4:
time: 107 us; the launch traced here: 106 us
  waiting for transfers between devices  47.5 us (44%)
  starting transfers between devices  28.1 us (26%)
  Pallas kernels  26.9 us (25%)
  local copies, waits for them, and re-layouts  1.83 us (2%)
    all_to_all x4, waiting for transfers between devices, exchange(): return lax.all_to_all(a, axes, split_axis=0, concat_axis=0, tiled=True)  47.4 us
    all_to_all x4, starting transfers between devices, exchange(): return lax.all_to_all(a, axes, split_axis=0, concat_axis=0, tiled=True)  26.5 us
    pallas_call x2, Pallas kernels, attention(): pl.pallas_call(functools.partial(attention_kernel, part), in_specs=[smem]...  22.6 us
    pallas_call x1, Pallas kernels, pack(): pl.pallas_call(pack_kernel, in_specs=[smem, smem] + [here] * 4, out_specs...  2.84 us
  transfers between devices with their start and end apart: 7, of which 4 were waited for; matrix products, arithmetic and copies ran while one was open for 1% of the time, Pallas kernels for 14%

profile of v4, /device:TPU:1, one launch (start us, length us, event | category | flops | bytes accessed | tf_op | source)
XLA Modules:
  0.0 106.1 jit_solution(1333298013078344939)
XLA Ops:
  0.6 1.4 %rows.1 = bf16[256,256]{1,0:T(8,128)(2,1)} custom-call(bf16[8,1024]{1,0:T(8,128)(2,1)} %key_ref.1, bf16[8,1024]{1,0:T(8,128)(2,1)} %value_ref.1), custom_call_target="tpu_custom_call" | custom-call | tf_op jit(solution)/shard_map/rows/pallas_call | solution.py:339
  2.0 12.8 %all-to-all-start = ((bf16[32,8,256]{2,1,0:T(8,128)(2,1)}), bf16[32,8,256]{2,1,0:T(8,128)(2,1)S(1)}, u32[]{:S(2)}, u32[]{:S(2)}) async-start(bf16[32,8,256]{2,1,0:T(8,128)(2,1)} %bitcast.12), calls=%async_computation | async-start | bytes 262144 | tf_op jit(solution)/shard_map/all_to_all | solution.py:261
  14.8 0.0 copy-start
  14.8 0.0 copy-start.3
  14.8 0.0 copy-start.4
  14.9 2.8 %pack.1 = (bf16[256,1536]{1,0:T(8,128)(2,1)}, f32[1,4]{1,0:T(1,128)}) custom-call(s32[1,2]{1,0:T(1,128)} %refs_0_.1, f32[1,2]{1,0:T(1,128)} %refs_1_.1, bf16[256,1280]{1,0:T(8,128)(2,1)} %refs_2_.1, bf16[256,1280]{1,0:T(8,128)(2,1)} %refs_3_.1, bf16[256,256]{1,0:T(8,128)(2,1)} %refs_4_.1, bf16[256,256]{1,0:T(8,128)(2,1)} %refs_5_.1), custom_call_target="tpu_custom_call" | custom-call | tf_op jit(solution)/shard_map/pack/pallas_call | solution.py:305
  17.7 7.8 %all-to-all-done = bf16[32,8,256]{2,1,0:T(8,128)(2,1)S(1)} async-done(((bf16[32,8,256]{2,1,0:T(8,128)(2,1)}), bf16[32,8,256]{2,1,0:T(8,128)(2,1)S(1)}, u32[]{:S(2)}, u32[]{:S(2)}) %all-to-all-start) | async-done | bytes 131104 | tf_op jit(solution)/shard_map/all_to_all | solution.py:261
  25.6 1.0 broadcast_in_dim.2
  26.6 4.1 %all-to-all-start.1 = ((bf16[8,256,256]{2,1,0:T(8,128)(2,1)}), bf16[8,256,256]{2,1,0:T(8,128)(2,1)S(1)}, u32[]{:S(2)}, u32[]{:S(2)}) async-start(bf16[8,256,256]{2,1,0:T(8,128)(2,1)} %broadcast_in_dim.2), calls=%async_computation.1 | async-start | bytes 2097152 | tf_op jit(solution)/shard_map/all_to_all | solution.py:261
  30.7 0.4 collective-permute-start.1
  31.1 1.1 %collective-permute-start = (f32[1,4]{1,0:T(1,128)S(1)}, f32[1,4]{1,0:T(1,128)S(1)}, u32[]{:S(2)}, u32[]{:S(2)}) collective-permute-start(f32[1,4]{1,0:T(1,128)S(1)} %copy-done.14), channel_id=1, source_target_pairs={{0,4},{4,0},{1,5},{5,1},{2,6},{6,2},{3,7},{7,3},{8,12},{12,8},{9,1... | collective-permute-start | bytes 56 | tf_op jit(solution)/shard_map/ppermute | solution.py:349
  32.2 14.5 %all-to-all-done.1 = bf16[8,256,256]{2,1,0:T(8,128)(2,1)S(1)} async-done(((bf16[8,256,256]{2,1,0:T(8,128)(2,1)}), bf16[8,256,256]{2,1,0:T(8,128)(2,1)S(1)}, u32[]{:S(2)}, u32[]{:S(2)}) %all-to-all-start.1) | async-done | bytes 1048608 | tf_op jit(solution)/shard_map/all_to_all | solution.py:261
  46.7 12.1 %attention.2 = (bf16[256,1280]{1,0:T(8,128)(2,1)}, bf16[256,256]{1,0:T(8,128)(2,1)}, bf16[256,256]{1,0:T(8,128)(2,1)}, f32[2048,256]{1,0:T(8,128)S(1)}) custom-call(s32[1,2]{1,0:T(1,128)S(1)} %copy-done.4, f32[1,2]{1,0:T(1,128)S(1)} %copy-done.5, bf16[256,1280]{1,0:T(8,128)(2,1)S(1)} %copy-done, bf16[256,1280]{1,0:T(8,128)(2,1)S(1)} %copy-done.1, ...), custom_call_target="tpu_custom_call" | custom-call | flops 4529848320 | bytes 4194304 | tf_op jit(solution)/shard_map/attention/pallas_call | solution.py:221
  58.9 10.5 %attention.3 = (bf16[256,896]{1,0:T(8,128)(2,1)S(1)}, bf16[2048,256]{1,0:T(8,128)(2,1)}) custom-call(f32[1,4]{1,0:T(1,128)S(1)} %collective-permute-done.refs_0_, bf16[256,1536]{1,0:T(8,128)(2,1)S(1)} %collective-permute-done.1.refs_1_, bf16[2048,256]{1,0:T(8,128)(2,1)S(1)} %bitcast.10, f32[2048,256]{1,0:T(8,128)S(1)} %get-tuple-element.22.refs_3_), custom_call_target="tpu_custom_call" | custom-call | flops 4529848320 | bytes 4194304 | tf_op jit(solution)/shard_map/attention/pallas_call | solution.py:221
  69.4 0.0 copy-start.12
  69.4 3.7 %all-to-all-start.2 = ((bf16[8,256,256]{2,1,0:T(8,128)(2,1)}), bf16[8,256,256]{2,1,0:T(8,128)(2,1)S(1)}, u32[]{:S(2)}, u32[]{:S(2)}) async-start(bf16[8,256,256]{2,1,0:T(8,128)(2,1)} %bitcast.3), calls=%async_computation.2 | async-start | bytes 2097152 | tf_op jit(solution)/shard_map/all_to_all | solution.py:261
  73.1 0.1 collective-permute-start.2
  73.3 14.5 %all-to-all-done.2 = bf16[8,256,256]{2,1,0:T(8,128)(2,1)S(1)} async-done(((bf16[8,256,256]{2,1,0:T(8,128)(2,1)}), bf16[8,256,256]{2,1,0:T(8,128)(2,1)S(1)}, u32[]{:S(2)}, u32[]{:S(2)}) %all-to-all-start.2) | async-done | bytes 1048608 | tf_op jit(solution)/shard_map/all_to_all | solution.py:261
  87.8 0.8 reduce_sum.21
  88.6 5.9 %all-to-all-start.3 = ((bf16[32,8,256]{2,1,0:T(8,128)(2,1)}), bf16[32,8,256]{2,1,0:T(8,128)(2,1)S(1)}, u32[]{:S(2)}, u32[]{:S(2)}) async-start(bf16[32,8,256]{2,1,0:T(8,128)(2,1)} %bitcast.4), calls=%async_computation.3 | async-start | bytes 262144 | tf_op jit(solution)/shard_map/all_to_all | solution.py:261
  94.7 10.6 %all-to-all-done.3 = bf16[32,8,256]{2,1,0:T(8,128)(2,1)S(1)} async-done(((bf16[32,8,256]{2,1,0:T(8,128)(2,1)}), bf16[32,8,256]{2,1,0:T(8,128)(2,1)S(1)}, u32[]{:S(2)}, u32[]{:S(2)}) %all-to-all-start.3) | async-done | bytes 131104 | tf_op jit(solution)/shard_map/all_to_all | solution.py:261
  105.4 0.0 copy-start.7
  105.5 0.6 copy-done.6
  106.0 0.0 copy-done.7
  (37 shorter events, 0.2 us)
Async XLA Ops:
  2.0 23.5 %all-to-all-start = ((bf16[32,8,256]{2,1,0:T(8,128)(2,1)}), bf16[32,8,256]{2,1,0:T(8,128)(2,1)S(1)}, u32[]{:S(2)}, u32[]{:S(2)}) async-start(bf16[32,8,256]{2,1,0:T(8,128)(2,1)} %bitcast.12), calls=%async_computation | async-start | bytes 262144 | tf_op jit(solution)/shard_map/all_to_all | solution.py:261
  14.8 31.9 %copy-start = (bf16[256,1280]{1,0:T(8,128)(2,1)S(1)}, bf16[256,1280]{1,0:T(8,128)(2,1)}, u32[]{:S(2)}) copy-start(bf16[256,1280]{1,0:T(8,128)(2,1)} %refs_2_.1) | copy-start | bytes 1966084
  14.8 31.9 %copy-start.1 = (bf16[256,1280]{1,0:T(8,128)(2,1)S(1)}, bf16[256,1280]{1,0:T(8,128)(2,1)}, u32[]{:S(2)}) copy-start(bf16[256,1280]{1,0:T(8,128)(2,1)} %refs_3_.1) | copy-start | bytes 1966084
  14.8 31.9 %copy-start.2 = (bf16[256,256]{1,0:T(8,128)(2,1)S(1)}, bf16[256,256]{1,0:T(8,128)(2,1)}, u32[]{:S(2)}) copy-start(bf16[256,256]{1,0:T(8,128)(2,1)} %refs_4_.1) | copy-start | bytes 393220
  14.8 31.9 %copy-start.3 = (bf16[256,256]{1,0:T(8,128)(2,1)S(1)}, bf16[256,256]{1,0:T(8,128)(2,1)}, u32[]{:S(2)}) copy-start(bf16[256,256]{1,0:T(8,128)(2,1)} %refs_5_.1) | copy-start | bytes 393220
  14.8 31.9 %copy-start.4 = (s32[1,2]{1,0:T(1,128)S(1)}, s32[1,2]{1,0:T(1,128)}, u32[]{:S(2)}) copy-start(s32[1,2]{1,0:T(1,128)} %refs_0_.1) | copy-start | bytes 28
  14.9 31.9 %copy-start.5 = (f32[1,2]{1,0:T(1,128)S(1)}, f32[1,2]{1,0:T(1,128)}, u32[]{:S(2)}) copy-start(f32[1,2]{1,0:T(1,128)} %refs_1_.1) | copy-start | bytes 28
  17.7 13.4 %copy-start.14 = (f32[1,4]{1,0:T(1,128)S(1)}, f32[1,4]{1,0:T(1,128)}, u32[]{:S(2)}) copy-start(f32[1,4]{1,0:T(1,128)} %get-tuple-element.20) | copy-start | bytes 52
  26.6 20.1 %all-to-all-start.1 = ((bf16[8,256,256]{2,1,0:T(8,128)(2,1)}), bf16[8,256,256]{2,1,0:T(8,128)(2,1)S(1)}, u32[]{:S(2)}, u32[]{:S(2)}) async-start(bf16[8,256,256]{2,1,0:T(8,128)(2,1)} %broadcast_in_dim.2), calls=%async_computation.1 | async-start | bytes 2097152 | tf_op jit(solution)/shard_map/all_to_all | solution.py:261
  30.7 28.2 %collective-permute-start.1 = (bf16[256,1536]{1,0:T(8,128)(2,1)}, bf16[256,1536]{1,0:T(8,128)(2,1)S(1)}, u32[]{:S(2)}, u32[]{:S(2)}) collective-permute-start(bf16[256,1536]{1,0:T(8,128)(2,1)} %get-tuple-element.21), channel_id=1, source_target_pairs={{0,4},{4,0},{1,5},{5,1},{2,6},{6,2},{3,7},{7,3},{8,12},{12,8},{9,1... | collective-permute-start | bytes 2359304 | tf_op jit(solution)/shard_map/ppermute | solution.py:348
  31.1 27.8 %collective-permute-start = (f32[1,4]{1,0:T(1,128)S(1)}, f32[1,4]{1,0:T(1,128)S(1)}, u32[]{:S(2)}, u32[]{:S(2)}) collective-permute-start(f32[1,4]{1,0:T(1,128)S(1)} %copy-done.14), channel_id=1, source_target_pairs={{0,4},{4,0},{1,5},{5,1},{2,6},{6,2},{3,7},{7,3},{8,12},{12,8},{9,1... | collective-permute-start | bytes 56 | tf_op jit(solution)/shard_map/ppermute | solution.py:349
  69.4 25.2 %copy-start.10 = (bf16[256,256]{1,0:T(8,128)(2,1)S(1)}, bf16[256,256]{1,0:T(8,128)(2,1)}, u32[]{:S(2)}) copy-start(bf16[256,256]{1,0:T(8,128)(2,1)} %get-tuple-element.24) | copy-start | bytes 393220
  69.4 25.2 %copy-start.12 = (bf16[256,256]{1,0:T(8,128)(2,1)S(1)}, bf16[256,256]{1,0:T(8,128)(2,1)}, u32[]{:S(2)}) copy-start(bf16[256,256]{1,0:T(8,128)(2,1)} %get-tuple-element.25) | copy-start | bytes 393220
  69.4 25.2 %copy-start.8 = (bf16[256,1280]{1,0:T(8,128)(2,1)S(1)}, bf16[256,1280]{1,0:T(8,128)(2,1)}, u32[]{:S(2)}) copy-start(bf16[256,1280]{1,0:T(8,128)(2,1)} %get-tuple-element.19) | copy-start | bytes 1966084
  69.4 18.3 %all-to-all-start.2 = ((bf16[8,256,256]{2,1,0:T(8,128)(2,1)}), bf16[8,256,256]{2,1,0:T(8,128)(2,1)S(1)}, u32[]{:S(2)}, u32[]{:S(2)}) async-start(bf16[8,256,256]{2,1,0:T(8,128)(2,1)} %bitcast.3), calls=%async_computation.2 | async-start | bytes 2097152 | tf_op jit(solution)/shard_map/all_to_all | solution.py:261
  73.1 21.4 %collective-permute-start.2 = (bf16[256,896]{1,0:T(8,128)(2,1)S(1)}, bf16[256,896]{1,0:T(8,128)(2,1)S(1)}, u32[]{:S(2)}, u32[]{:S(2)}) collective-permute-start(bf16[256,896]{1,0:T(8,128)(2,1)S(1)} %get-tuple-element.23), channel_id=1, source_target_pairs={{0,4},{4,0},{1,5},{5,1},{2,6},{6,2},{3,7},{7,3},{8,12},{12,8},{9,1... | collective-permute-start | bytes 1376264 | tf_op jit(solution)/shard_map/ppermute | solution.py:362
  88.6 16.7 %all-to-all-start.3 = ((bf16[32,8,256]{2,1,0:T(8,128)(2,1)}), bf16[32,8,256]{2,1,0:T(8,128)(2,1)S(1)}, u32[]{:S(2)}, u32[]{:S(2)}) async-start(bf16[32,8,256]{2,1,0:T(8,128)(2,1)} %bitcast.4), calls=%async_computation.3 | async-start | bytes 262144 | tf_op jit(solution)/shard_map/all_to_all | solution.py:261
  94.6 10.8 %copy-start.11 = (bf16[256,256]{1,0:T(8,128)(2,1)}, bf16[256,256]{1,0:T(8,128)(2,1)S(1)}, u32[]{:S(2)}) copy-start(bf16[256,256]{1,0:T(8,128)(2,1)S(1)} %get-tuple-element.28) | copy-start | bytes 393220
  94.6 10.8 %copy-start.13 = (bf16[256,256]{1,0:T(8,128)(2,1)}, bf16[256,256]{1,0:T(8,128)(2,1)S(1)}, u32[]{:S(2)}) copy-start(bf16[256,256]{1,0:T(8,128)(2,1)S(1)} %get-tuple-element.27) | copy-start | bytes 393220
  94.7 10.8 %copy-start.9 = (bf16[256,1280]{1,0:T(8,128)(2,1)}, bf16[256,1280]{1,0:T(8,128)(2,1)S(1)}, u32[]{:S(2)}) copy-start(bf16[256,1280]{1,0:T(8,128)(2,1)S(1)} %slice_dynamic-update-slice_fusion) | copy-start | bytes 1966084
  105.4 0.6 copy-start.6
  105.4 0.6 copy-start.7

commit v5 on v4

--- a/solution.py
+++ b/solution.py
@@ -13,7 +13,7 @@
 KEY_VALUE_HEADS = 8
 HEAD = 128
 GROUP = QUERY_HEADS // KEY_VALUE_HEADS
-CHUNK = 512
+CHUNKS = (1024, 2048)
 FOLD = 16
 PROMPT_TOKENS = 2048
 VMEM_MIB = 38
@@ -45,7 +45,8 @@
      peak_ref, sum_ref, dot_ref, in_sem, kv_sem, out_sem) = refs[-17:]
     tokens = tok_ref.shape[0]
     prompt = kv_ref.shape[0]
-    chunks = prompt // CHUNK
+    chunk = CHUNKS[part]
+    chunks = prompt // chunk
     factor = 1.0 / math.sqrt(HEAD)
     scale = factor * LOG2E
 
@@ -65,7 +66,7 @@
         copy.start()
     kv_loads, sum_loads = [], []
     for c in range(chunks):
-        at = pl.ds(c * CHUNK, CHUNK)
+        at = pl.ds(c * chunk, chunk)
         kv_loads.append(pltpu.make_async_copy(kv_hbm.at[at], kv_ref.at[at], kv_sem.at[c]))
         kv_loads[-1].start()
     if part == 1:
@@ -166,10 +167,10 @@
     kt_ref[:, prompt:] = turn(near_keys)
     forward(near_keys, tok_ref[:, V_COLS], prompt, near)
     for c in range(chunks):
-        at = slice(c * CHUNK, (c + 1) * CHUNK)
+        at = slice(c * chunk, (c + 1) * chunk)
         kv_loads[c].wait()
         kt_ref[:, at] = turn(kv_ref[at, :HEAD])
-        forward(kv_ref[at, :HEAD], kv_ref[at, HEAD:], c * CHUNK, None)
+        forward(kv_ref[at, :HEAD], kv_ref[at, HEAD:], c * chunk, None)
 
     deltas = []
     for g in range(GROUP):
@@ -188,9 +189,9 @@
     grad_ref[:, GK_COLS] = key_grad.astype(jnp.bfloat16)
     grad_ref[:, GV_COLS] = value_grad.astype(jnp.bfloat16)
     for c in range(chunks):
-        at = slice(c * CHUNK, (c + 1) * CHUNK)
-        block = pl.ds(c * CHUNK, CHUNK)
-        key_grad, value_grad = backward(c * CHUNK, CHUNK, deltas)
+        at = slice(c * chunk, (c + 1) * chunk)
+        block = pl.ds(c * chunk, chunk)
+        key_grad, value_grad = backward(c * chunk, chunk, deltas)
         if part == 0:
             sum_kv_ref[at, :HEAD], sum_kv_ref[at, HEAD:] = key_grad, value_grad
             store(sum_kv_ref.at[block], sum_hbm.at[block])
@@ -215,6 +216,7 @@
     prompt = PROMPT_TOKENS
     span = prompt + tokens
     wide = GROUP * tokens
+    chunks = prompt // CHUNKS[part]
     smem = pl.BlockSpec(memory_space=pltpu.SMEM)
     here = pl.BlockSpec(memory_space=pl.ANY)
     bf16, f32 = jnp.bfloat16, jnp.float32
@@ -239,8 +241,8 @@
             pltpu.VMEM((span // FOLD, wide), f32),
             pltpu.VMEM((span // FOLD, wide), f32),
             pltpu.SemaphoreType.DMA((4,)),
-            pltpu.SemaphoreType.DMA((prompt // CHUNK,)),
-            pltpu.SemaphoreType.DMA((prompt // CHUNK + 3,)),
+            pltpu.SemaphoreType.DMA((chunks,)),
+            pltpu.SemaphoreType.DMA((chunks + 3,)),
         ],
         compiler_params=pltpu.CompilerParams(vmem_limit_bytes=VMEM_MIB * 1024 * 1024),
         cost_estimate=pl.CostEstimate(

time: 107 us -> 105 us (0.981)
  Pallas kernels: 26.9 us -> 25 us
    pallas_call x2, Pallas kernels: 22.6 us -> 20.8 us  [attention(): pl.pallas_call(functools.partial(attention_kernel, part), in_specs=[smem]...]
  transfers between devices with their start and end apart: 7 -> 7, of which waited for: 4 -> 4; matrix products, arithmetic and copies ran while one was open for 1% -> 1% of each run, Pallas kernels for 14% -> 13%
where the time goes in v5:
time: 105 us; the launch traced here: 104 us
  waiting for transfers between devices  47.4 us (45%)
  starting transfers between devices  28.1 us (27%)
  Pallas kernels  25 us (24%)
  local copies, waits for them, and re-layouts  1.83 us (2%)
    all_to_all x4, waiting for transfers between devices, exchange(): return lax.all_to_all(a, axes, split_axis=0, concat_axis=0, tiled=True)  47.4 us
    all_to_all x4, starting transfers between devices, exchange(): return lax.all_to_all(a, axes, split_axis=0, concat_axis=0, tiled=True)  26.6 us
    pallas_call x2, Pallas kernels, attention(): pl.pallas_call(functools.partial(attention_kernel, part), in_specs=[smem]...  20.8 us
    pallas_call x1, Pallas kernels, pack(): pl.pallas_call(pack_kernel, in_specs=[smem, smem] + [here] * 4, out_specs...  2.84 us
  transfers between devices with their start and end apart: 7, of which 4 were waited for; matrix products, arithmetic and copies ran while one was open for 1% of the time, Pallas kernels for 13%

profile of v5, /device:TPU:1, one launch (start us, length us, event | category | flops | bytes accessed | tf_op | source)
XLA Modules:
  0.0 104.2 jit_solution(8329334507521431677)
XLA Ops:
  0.6 1.4 %rows.1 = bf16[256,256]{1,0:T(8,128)(2,1)} custom-call(bf16[8,1024]{1,0:T(8,128)(2,1)} %key_ref.1, bf16[8,1024]{1,0:T(8,128)(2,1)} %value_ref.1), custom_call_target="tpu_custom_call" | custom-call | tf_op jit(solution)/shard_map/rows/pallas_call | solution.py:341
  2.0 12.8 %all-to-all-start = ((bf16[32,8,256]{2,1,0:T(8,128)(2,1)}), bf16[32,8,256]{2,1,0:T(8,128)(2,1)S(1)}, u32[]{:S(2)}, u32[]{:S(2)}) async-start(bf16[32,8,256]{2,1,0:T(8,128)(2,1)} %bitcast.12), calls=%async_computation | async-start | bytes 262144 | tf_op jit(solution)/shard_map/all_to_all | solution.py:263
  14.8 0.0 copy-start
  14.8 0.0 copy-start.3
  14.8 0.0 copy-start.4
  14.9 2.8 %pack.1 = (bf16[256,1536]{1,0:T(8,128)(2,1)}, f32[1,4]{1,0:T(1,128)}) custom-call(s32[1,2]{1,0:T(1,128)} %refs_0_.1, f32[1,2]{1,0:T(1,128)} %refs_1_.1, bf16[256,1280]{1,0:T(8,128)(2,1)} %refs_2_.1, bf16[256,1280]{1,0:T(8,128)(2,1)} %refs_3_.1, bf16[256,256]{1,0:T(8,128)(2,1)} %refs_4_.1, bf16[256,256]{1,0:T(8,128)(2,1)} %refs_5_.1), custom_call_target="tpu_custom_call" | custom-call | tf_op jit(solution)/shard_map/pack/pallas_call | solution.py:307
  17.7 7.8 %all-to-all-done = bf16[32,8,256]{2,1,0:T(8,128)(2,1)S(1)} async-done(((bf16[32,8,256]{2,1,0:T(8,128)(2,1)}), bf16[32,8,256]{2,1,0:T(8,128)(2,1)S(1)}, u32[]{:S(2)}, u32[]{:S(2)}) %all-to-all-start) | async-done | bytes 131104 | tf_op jit(solution)/shard_map/all_to_all | solution.py:263
  25.6 1.0 %broadcast_in_dim.2 = bf16[8,256,256]{2,1,0:T(8,128)(2,1)} broadcast(bf16[256,256]{1,0:T(8,128)(2,1)S(1)} %bitcast.11), dimensions={1,2} | broadcast | bytes 1179648 | tf_op jit(solution)/shard_map/broadcast_in_dim | solution.py:352
  26.6 4.1 %all-to-all-start.1 = ((bf16[8,256,256]{2,1,0:T(8,128)(2,1)}), bf16[8,256,256]{2,1,0:T(8,128)(2,1)S(1)}, u32[]{:S(2)}, u32[]{:S(2)}) async-start(bf16[8,256,256]{2,1,0:T(8,128)(2,1)} %broadcast_in_dim.2), calls=%async_computation.1 | async-start | bytes 2097152 | tf_op jit(solution)/shard_map/all_to_all | solution.py:263
  30.7 0.4 collective-permute-start.1
  31.1 1.1 %collective-permute-start = (f32[1,4]{1,0:T(1,128)S(1)}, f32[1,4]{1,0:T(1,128)S(1)}, u32[]{:S(2)}, u32[]{:S(2)}) collective-permute-start(f32[1,4]{1,0:T(1,128)S(1)} %copy-done.14), channel_id=1, source_target_pairs={{0,4},{4,0},{1,5},{5,1},{2,6},{6,2},{3,7},{7,3},{8,12},{12,8},{9,1... | collective-permute-start | bytes 56 | tf_op jit(solution)/shard_map/ppermute | solution.py:351
  32.2 14.5 %all-to-all-done.1 = bf16[8,256,256]{2,1,0:T(8,128)(2,1)S(1)} async-done(((bf16[8,256,256]{2,1,0:T(8,128)(2,1)}), bf16[8,256,256]{2,1,0:T(8,128)(2,1)S(1)}, u32[]{:S(2)}, u32[]{:S(2)}) %all-to-all-start.1) | async-done | bytes 1048608 | tf_op jit(solution)/shard_map/all_to_all | solution.py:263
  46.7 10.6 %attention.2 = (bf16[256,1280]{1,0:T(8,128)(2,1)}, bf16[256,256]{1,0:T(8,128)(2,1)}, bf16[256,256]{1,0:T(8,128)(2,1)}, f32[2048,256]{1,0:T(8,128)S(1)}) custom-call(s32[1,2]{1,0:T(1,128)S(1)} %copy-done.4, f32[1,2]{1,0:T(1,128)S(1)} %copy-done.5, bf16[256,1280]{1,0:T(8,128)(2,1)S(1)} %copy-done, bf16[256,1280]{1,0:T(8,128)(2,1)S(1)} %copy-done.1, ...), custom_call_target="tpu_custom_call" | custom-call | flops 4529848320 | bytes 4194304 | tf_op jit(solution)/shard_map/attention/pallas_call | solution.py:223
  57.4 10.2 %attention.3 = (bf16[256,896]{1,0:T(8,128)(2,1)S(1)}, bf16[2048,256]{1,0:T(8,128)(2,1)}) custom-call(f32[1,4]{1,0:T(1,128)S(1)} %collective-permute-done.refs_0_, bf16[256,1536]{1,0:T(8,128)(2,1)S(1)} %collective-permute-done.1.refs_1_, bf16[2048,256]{1,0:T(8,128)(2,1)S(1)} %bitcast.10, f32[2048,256]{1,0:T(8,128)S(1)} %get-tuple-element.22.refs_3_), custom_call_target="tpu_custom_call" | custom-call | flops 4529848320 | bytes 4194304 | tf_op jit(solution)/shard_map/attention/pallas_call | solution.py:223
  67.6 0.0 copy-start.8
  67.6 3.7 %all-to-all-start.2 = ((bf16[8,256,256]{2,1,0:T(8,128)(2,1)}), bf16[8,256,256]{2,1,0:T(8,128)(2,1)S(1)}, u32[]{:S(2)}, u32[]{:S(2)}) async-start(bf16[8,256,256]{2,1,0:T(8,128)(2,1)} %bitcast.3), calls=%async_computation.2 | async-start | bytes 2097152 | tf_op jit(solution)/shard_map/all_to_all | solution.py:263
  71.3 0.1 collective-permute-start.2
  71.4 14.5 %all-to-all-done.2 = bf16[8,256,256]{2,1,0:T(8,128)(2,1)S(1)} async-done(((bf16[8,256,256]{2,1,0:T(8,128)(2,1)}), bf16[8,256,256]{2,1,0:T(8,128)(2,1)S(1)}, u32[]{:S(2)}, u32[]{:S(2)}) %all-to-all-start.2) | async-done | bytes 1048608 | tf_op jit(solution)/shard_map/all_to_all | solution.py:263
  85.9 0.8 reduce_sum.21
  86.7 6.0 %all-to-all-start.3 = ((bf16[32,8,256]{2,1,0:T(8,128)(2,1)}), bf16[32,8,256]{2,1,0:T(8,128)(2,1)S(1)}, u32[]{:S(2)}, u32[]{:S(2)}) async-start(bf16[32,8,256]{2,1,0:T(8,128)(2,1)} %bitcast.4), calls=%async_computation.3 | async-start | bytes 262144 | tf_op jit(solution)/shard_map/all_to_all | solution.py:263
  92.9 10.6 %all-to-all-done.3 = bf16[32,8,256]{2,1,0:T(8,128)(2,1)S(1)} async-done(((bf16[32,8,256]{2,1,0:T(8,128)(2,1)}), bf16[32,8,256]{2,1,0:T(8,128)(2,1)S(1)}, u32[]{:S(2)}, u32[]{:S(2)}) %all-to-all-start.3) | async-done | bytes 131104 | tf_op jit(solution)/shard_map/all_to_all | solution.py:263
  103.6 0.0 copy-start.7
  103.7 0.6 copy-done.6
  104.2 0.0 copy-done.7
  (37 shorter events, 0.2 us)
Async XLA Ops:
  2.0 23.5 %all-to-all-start = ((bf16[32,8,256]{2,1,0:T(8,128)(2,1)}), bf16[32,8,256]{2,1,0:T(8,128)(2,1)S(1)}, u32[]{:S(2)}, u32[]{:S(2)}) async-start(bf16[32,8,256]{2,1,0:T(8,128)(2,1)} %bitcast.12), calls=%async_computation | async-start | bytes 262144 | tf_op jit(solution)/shard_map/all_to_all | solution.py:263
  14.8 31.9 %copy-start = (bf16[256,1280]{1,0:T(8,128)(2,1)S(1)}, bf16[256,1280]{1,0:T(8,128)(2,1)}, u32[]{:S(2)}) copy-start(bf16[256,1280]{1,0:T(8,128)(2,1)} %refs_2_.1) | copy-start | bytes 1966084
  14.8 31.9 %copy-start.1 = (bf16[256,1280]{1,0:T(8,128)(2,1)S(1)}, bf16[256,1280]{1,0:T(8,128)(2,1)}, u32[]{:S(2)}) copy-start(bf16[256,1280]{1,0:T(8,128)(2,1)} %refs_3_.1) | copy-start | bytes 1966084
  14.8 31.9 %copy-start.2 = (bf16[256,256]{1,0:T(8,128)(2,1)S(1)}, bf16[256,256]{1,0:T(8,128)(2,1)}, u32[]{:S(2)}) copy-start(bf16[256,256]{1,0:T(8,128)(2,1)} %refs_4_.1) | copy-start | bytes 393220
  14.8 31.9 %copy-start.3 = (bf16[256,256]{1,0:T(8,128)(2,1)S(1)}, bf16[256,256]{1,0:T(8,128)(2,1)}, u32[]{:S(2)}) copy-start(bf16[256,256]{1,0:T(8,128)(2,1)} %refs_5_.1) | copy-start | bytes 393220
  14.8 31.9 %copy-start.4 = (s32[1,2]{1,0:T(1,128)S(1)}, s32[1,2]{1,0:T(1,128)}, u32[]{:S(2)}) copy-start(s32[1,2]{1,0:T(1,128)} %refs_0_.1) | copy-start | bytes 28
  14.9 31.9 %copy-start.5 = (f32[1,2]{1,0:T(1,128)S(1)}, f32[1,2]{1,0:T(1,128)}, u32[]{:S(2)}) copy-start(f32[1,2]{1,0:T(1,128)} %refs_1_.1) | copy-start | bytes 28
  17.7 13.4 %copy-start.14 = (f32[1,4]{1,0:T(1,128)S(1)}, f32[1,4]{1,0:T(1,128)}, u32[]{:S(2)}) copy-start(f32[1,4]{1,0:T(1,128)} %get-tuple-element.20) | copy-start | bytes 52
  26.6 20.1 %all-to-all-start.1 = ((bf16[8,256,256]{2,1,0:T(8,128)(2,1)}), bf16[8,256,256]{2,1,0:T(8,128)(2,1)S(1)}, u32[]{:S(2)}, u32[]{:S(2)}) async-start(bf16[8,256,256]{2,1,0:T(8,128)(2,1)} %broadcast_in_dim.2), calls=%async_computation.1 | async-start | bytes 2097152 | tf_op jit(solution)/shard_map/all_to_all | solution.py:263
  30.7 26.6 %collective-permute-start.1 = (bf16[256,1536]{1,0:T(8,128)(2,1)}, bf16[256,1536]{1,0:T(8,128)(2,1)S(1)}, u32[]{:S(2)}, u32[]{:S(2)}) collective-permute-start(bf16[256,1536]{1,0:T(8,128)(2,1)} %get-tuple-element.21), channel_id=1, source_target_pairs={{0,4},{4,0},{1,5},{5,1},{2,6},{6,2},{3,7},{7,3},{8,12},{12,8},{9,1... | collective-permute-start | bytes 2359304 | tf_op jit(solution)/shard_map/ppermute | solution.py:350
  31.1 26.2 %collective-permute-start = (f32[1,4]{1,0:T(1,128)S(1)}, f32[1,4]{1,0:T(1,128)S(1)}, u32[]{:S(2)}, u32[]{:S(2)}) collective-permute-start(f32[1,4]{1,0:T(1,128)S(1)} %copy-done.14), channel_id=1, source_target_pairs={{0,4},{4,0},{1,5},{5,1},{2,6},{6,2},{3,7},{7,3},{8,12},{12,8},{9,1... | collective-permute-start | bytes 56 | tf_op jit(solution)/shard_map/ppermute | solution.py:351
  67.6 25.2 %copy-start.10 = (bf16[256,256]{1,0:T(8,128)(2,1)S(1)}, bf16[256,256]{1,0:T(8,128)(2,1)}, u32[]{:S(2)}) copy-start(bf16[256,256]{1,0:T(8,128)(2,1)} %get-tuple-element.24) | copy-start | bytes 393220
  67.6 25.2 %copy-start.12 = (bf16[256,256]{1,0:T(8,128)(2,1)S(1)}, bf16[256,256]{1,0:T(8,128)(2,1)}, u32[]{:S(2)}) copy-start(bf16[256,256]{1,0:T(8,128)(2,1)} %get-tuple-element.25) | copy-start | bytes 393220
  67.6 25.2 %copy-start.8 = (bf16[256,1280]{1,0:T(8,128)(2,1)S(1)}, bf16[256,1280]{1,0:T(8,128)(2,1)}, u32[]{:S(2)}) copy-start(bf16[256,1280]{1,0:T(8,128)(2,1)} %get-tuple-element.19) | copy-start | bytes 1966084
  67.6 18.3 %all-to-all-start.2 = ((bf16[8,256,256]{2,1,0:T(8,128)(2,1)}), bf16[8,256,256]{2,1,0:T(8,128)(2,1)S(1)}, u32[]{:S(2)}, u32[]{:S(2)}) async-start(bf16[8,256,256]{2,1,0:T(8,128)(2,1)} %bitcast.3), calls=%async_computation.2 | async-start | bytes 2097152 | tf_op jit(solution)/shard_map/all_to_all | solution.py:263
  71.3 21.4 %collective-permute-start.2 = (bf16[256,896]{1,0:T(8,128)(2,1)S(1)}, bf16[256,896]{1,0:T(8,128)(2,1)S(1)}, u32[]{:S(2)}, u32[]{:S(2)}) collective-permute-start(bf16[256,896]{1,0:T(8,128)(2,1)S(1)} %get-tuple-element.23), channel_id=1, source_target_pairs={{0,4},{4,0},{1,5},{5,1},{2,6},{6,2},{3,7},{7,3},{8,12},{12,8},{9,1... | collective-permute-start | bytes 1376264 | tf_op jit(solution)/shard_map/ppermute | solution.py:364
  86.7 16.7 %all-to-all-start.3 = ((bf16[32,8,256]{2,1,0:T(8,128)(2,1)}), bf16[32,8,256]{2,1,0:T(8,128)(2,1)S(1)}, u32[]{:S(2)}, u32[]{:S(2)}) async-start(bf16[32,8,256]{2,1,0:T(8,128)(2,1)} %bitcast.4), calls=%async_computation.3 | async-start | bytes 262144 | tf_op jit(solution)/shard_map/all_to_all | solution.py:263
  92.8 10.8 %copy-start.11 = (bf16[256,256]{1,0:T(8,128)(2,1)}, bf16[256,256]{1,0:T(8,128)(2,1)S(1)}, u32[]{:S(2)}) copy-start(bf16[256,256]{1,0:T(8,128)(2,1)S(1)} %get-tuple-element.28) | copy-start | bytes 393220
  92.8 10.8 %copy-start.13 = (bf16[256,256]{1,0:T(8,128)(2,1)}, bf16[256,256]{1,0:T(8,128)(2,1)S(1)}, u32[]{:S(2)}) copy-start(bf16[256,256]{1,0:T(8,128)(2,1)S(1)} %get-tuple-element.27) | copy-start | bytes 393220
  92.9 10.8 %copy-start.9 = (bf16[256,1280]{1,0:T(8,128)(2,1)}, bf16[256,1280]{1,0:T(8,128)(2,1)S(1)}, u32[]{:S(2)}) copy-start(bf16[256,1280]{1,0:T(8,128)(2,1)S(1)} %slice_dynamic-update-slice_fusion) | copy-start | bytes 1966084
  103.6 0.6 copy-start.6
  103.6 0.6 copy-start.7

commit v6 on v5

--- a/solution.py
+++ b/solution.py
@@ -17,7 +17,6 @@
 FOLD = 16
 PROMPT_TOKENS = 2048
 VMEM_MIB = 38
-TIE = True
 HALF = (GROUP + 1) * HEAD
 Q_COLS = slice(0, GROUP * HEAD)
 K_COLS = slice(GROUP * HEAD, HALF)
@@ -34,15 +33,19 @@
     return lax.dot_general(a, b, dims, preferred_element_type=jnp.float32)
 
 
-def attention_kernel(part, *refs):
-    if part == 0:
-        len_ref, adv_ref, q_hbm, og_hbm, nk_hbm, nv_hbm, kv_hbm = refs[:7]
-        gq_hbm, gnk_hbm, gnv_hbm, sum_hbm = refs[7:11]
+def attention_kernel(part, prompt_side, token_side, *refs):
+    refs = list(refs)
+    take = functools.partial(refs.pop, 0)
+    len_ref, tok_hbm, kv_hbm = take(), take(), take()
+    if part == 1:
+        sum_hbm, back_hbm, gkv_hbm = take(), take(), take()
+    elif token_side:
+        gq_hbm, gnk_hbm, gnv_hbm = take(), take(), take()
     else:
-        got_ref, got_hbm, kv_hbm, sum_hbm, back_hbm, gkv_hbm = refs[:6]
+        sum_hbm = take()
     (tok_ref, kv_ref, grad_ref, gkv_ref, sum_kv_ref,
      p_ref, d_ref, kt_ref, qt_ref, dot_t_ref, gqt_ref,
-     peak_ref, sum_ref, dot_ref, in_sem, kv_sem, out_sem) = refs[-17:]
+     peak_ref, sum_ref, dot_ref, in_sem, kv_sem, out_sem) = refs
     tokens = tok_ref.shape[0]
     prompt = kv_ref.shape[0]
     chunk = CHUNKS[part]
@@ -54,14 +57,7 @@
         mine = lax.axis_index("zl")
         query_cols = pl.ds(pl.multiple_of(mine * (GROUP * HEAD), HEAD), GROUP * HEAD)
         own_cols = pl.ds(pl.multiple_of(mine * HEAD, HEAD), HEAD)
-        loads = [
-            pltpu.make_async_copy(q_hbm.at[:, query_cols], tok_ref.at[:, Q_COLS], in_sem.at[0]),
-            pltpu.make_async_copy(og_hbm.at[:, query_cols], tok_ref.at[:, O_COLS], in_sem.at[1]),
-            pltpu.make_async_copy(nk_hbm.at[:, own_cols], tok_ref.at[:, K_COLS], in_sem.at[2]),
-            pltpu.make_async_copy(nv_hbm.at[:, own_cols], tok_ref.at[:, V_COLS], in_sem.at[3]),
-        ]
-    else:
-        loads = [pltpu.make_async_copy(got_hbm, tok_ref, in_sem.at[0])]
+    loads = [pltpu.make_async_copy(tok_hbm, tok_ref, in_sem.at[0])]
     for copy in loads:
         copy.start()
     kv_loads, sum_loads = [], []
@@ -112,6 +108,7 @@
     def backward(row, size, deltas):
         groups = size // (8 * FOLD)
         slot = row // FOLD
+        near = row == prompt
         key_sum = jnp.zeros((size, HEAD), jnp.float32)
         value_sum = jnp.zeros((size, HEAD), jnp.float32)
         for g in range(GROUP):
@@ -120,15 +117,17 @@
             share = peak_ref[slot:slot + 8 * groups, tok_cols(g)].reshape(groups, 1, 8, tokens)
             p = p * share
             ds = p * (d - deltas[g][None, None])
-            p = p.reshape(size, tokens).astype(jnp.bfloat16)
             ds = ds.reshape(size, tokens).astype(jnp.bfloat16)
-            key_sum = key_sum + dot(ds, tok_ref[:, head_cols(g)], NN)
-            value_sum = value_sum + dot(p, tok_ref[:, head_cols(g, HALF)], NN)
-            query_sum = dot(kt_ref[:, row:row + size], ds, NN)
-            if row == kt_ref.shape[1] - tokens:
-                gqt_ref[:, tok_cols(g)] = query_sum
-            else:
-                gqt_ref[:, tok_cols(g)] += query_sum
+            if near or prompt_side:
+                p = p.reshape(size, tokens).astype(jnp.bfloat16)
+                key_sum = key_sum + dot(ds, tok_ref[:, head_cols(g)], NN)
+                value_sum = value_sum + dot(p, tok_ref[:, head_cols(g, HALF)], NN)
+            if token_side:
+                query_sum = dot(kt_ref[:, row:row + size], ds, NN)
+                if near:
+                    gqt_ref[:, tok_cols(g)] = query_sum
+                else:
+                    gqt_ref[:, tok_cols(g)] += query_sum
         return key_sum * factor, value_sum
 
     stores = []
@@ -137,25 +136,11 @@
         stores.append(pltpu.make_async_copy(source, target, out_sem.at[len(stores)]))
         stores[-1].start()
 
-    if part == 0:
-        responses = len_ref.shape[1]
-        lengths = [len_ref[0, r] for r in range(responses)]
-        advantages = [adv_ref[0, r] for r in range(responses)]
-    else:
-        responses = got_ref.shape[1] // 2
-        lengths = [got_ref[0, r].astype(jnp.int32) for r in range(responses)]
-        advantages = [got_ref[0, responses + r] for r in range(responses)]
+    responses = len_ref.shape[1]
+    lengths = [len_ref[0, r] for r in range(responses)]
     ends = [sum(lengths[:r + 1]) for r in range(responses)]
     for copy in loads:
         copy.wait()
-    tok_seg = segment(lax.broadcasted_iota(jnp.int32, (tokens, HEAD), 0), ends)
-    weight = jnp.zeros((tokens, HEAD), jnp.float32)
-    for r in range(responses):
-        weight = jnp.where(tok_seg == r, advantages[r], weight)
-    for g in range(GROUP):
-        cols = head_cols(g, HALF)
-        do = weight * tok_ref[:, cols].astype(jnp.float32)
-        tok_ref[:, cols] = do.astype(jnp.bfloat16)
     for g in range(GROUP):
         qt_ref[:, tok_cols(g)] = turn(tok_ref[:, head_cols(g)])
         dot_t_ref[:, tok_cols(g)] = turn(tok_ref[:, head_cols(g, HALF)])
@@ -169,7 +154,8 @@
     for c in range(chunks):
         at = slice(c * chunk, (c + 1) * chunk)
         kv_loads[c].wait()
-        kt_ref[:, at] = turn(kv_ref[at, :HEAD])
+        if token_side:
+            kt_ref[:, at] = turn(kv_ref[at, :HEAD])
         forward(kv_ref[at, :HEAD], kv_ref[at, HEAD:], c * chunk, None)
 
     deltas = []
@@ -185,13 +171,16 @@
 
     for copy in sum_loads:
         copy.wait()
-    key_grad, value_grad = backward(prompt, tokens, deltas)
-    grad_ref[:, GK_COLS] = key_grad.astype(jnp.bfloat16)
-    grad_ref[:, GV_COLS] = value_grad.astype(jnp.bfloat16)
+    if token_side:
+        key_grad, value_grad = backward(prompt, tokens, deltas)
+        grad_ref[:, GK_COLS] = key_grad.astype(jnp.bfloat16)
+        grad_ref[:, GV_COLS] = value_grad.astype(jnp.bfloat16)
     for c in range(chunks):
         at = slice(c * chunk, (c + 1) * chunk)
         block = pl.ds(c * chunk, chunk)
         key_grad, value_grad = backward(c * chunk, chunk, deltas)
+        if not prompt_side:
+            continue
         if part == 0:
             sum_kv_ref[at, :HEAD], sum_kv_ref[at, HEAD:] = key_grad, value_grad
             store(sum_kv_ref.at[block], sum_hbm.at[block])
@@ -199,19 +188,20 @@
             gkv_ref[at, :HEAD] = (sum_kv_ref[at, :HEAD] + key_grad).astype(jnp.bfloat16)
             gkv_ref[at, HEAD:] = (sum_kv_ref[at, HEAD:] + value_grad).astype(jnp.bfloat16)
             store(gkv_ref.at[block], gkv_hbm.at[block])
-    for g in range(GROUP):
-        grad_ref[:, head_cols(g)] = (gqt_ref[:, tok_cols(g)].T * factor).astype(jnp.bfloat16)
-    if part == 0:
-        store(grad_ref.at[:, Q_COLS], gq_hbm.at[:, query_cols])
-        store(grad_ref.at[:, GK_COLS], gnk_hbm.at[:, own_cols])
-        store(grad_ref.at[:, GV_COLS], gnv_hbm.at[:, own_cols])
-    else:
-        store(grad_ref, back_hbm)
+    if token_side:
+        for g in range(GROUP):
+            grad_ref[:, head_cols(g)] = (gqt_ref[:, tok_cols(g)].T * factor).astype(jnp.bfloat16)
+        if part == 0:
+            store(grad_ref.at[:, Q_COLS], gq_hbm.at[:, query_cols])
+            store(grad_ref.at[:, GK_COLS], gnk_hbm.at[:, own_cols])
+            store(grad_ref.at[:, GV_COLS], gnv_hbm.at[:, own_cols])
+        else:
+            store(grad_ref, back_hbm)
     for copy in stores:
         copy.wait()
 
 
-def attention(part, smem_args, args, out_shape):
+def attention(part, prompt_side, token_side, smem_args, args, out_shape):
     tokens = args[0].shape[0]
     prompt = PROMPT_TOKENS
     span = prompt + tokens
@@ -221,7 +211,7 @@
     here = pl.BlockSpec(memory_space=pl.ANY)
     bf16, f32 = jnp.bfloat16, jnp.float32
     return pl.pallas_call(
-        functools.partial(attention_kernel, part),
+        functools.partial(attention_kernel, part, prompt_side, token_side),
         in_specs=[smem] * len(smem_args) + [here] * len(args),
         out_specs=[here] * len(out_shape),
         out_shape=out_shape,
@@ -280,39 +270,50 @@
         first_ref[c * count:(c + 1) * count, :] = rows
 
 
-def pack_kernel(len_ref, adv_ref, q_hbm, og_hbm, nk_hbm, nv_hbm, send_ref, scalars_ref, sem):
-    other = 1 - lax.axis_index("zl")
-    query_cols = pl.ds(pl.multiple_of(other * (GROUP * HEAD), HEAD), GROUP * HEAD)
-    key_cols = pl.ds(pl.multiple_of(other * HEAD, HEAD), HEAD)
-    moves = [
-        pltpu.make_async_copy(q_hbm.at[:, query_cols], send_ref.at[:, Q_COLS], sem.at[0]),
-        pltpu.make_async_copy(og_hbm.at[:, query_cols], send_ref.at[:, O_COLS], sem.at[1]),
-        pltpu.make_async_copy(nk_hbm.at[:, key_cols], send_ref.at[:, K_COLS], sem.at[2]),
-        pltpu.make_async_copy(nv_hbm.at[:, key_cols], send_ref.at[:, V_COLS], sem.at[3]),
-    ]
-    for move in moves:
-        move.start()
-    responses = len_ref.shape[1]
-    for r in range(responses):
-        scalars_ref[0, r] = len_ref[0, r].astype(jnp.float32)
-        scalars_ref[0, responses + r] = adv_ref[0, r]
-    for move in moves:
-        move.wait()
+def pack_kernel(
+    len_ref, adv_ref, q_hbm, og_hbm, nk_hbm, nv_hbm, own_ref, send_ref, sem
+):
+    mine = lax.axis_index("zl")
+    loads, late = [], []
+    for i, (head, held) in enumerate([(1 - mine, send_ref), (mine, own_ref)]):
+        query_cols = pl.ds(pl.multiple_of(head * (GROUP * HEAD), HEAD), GROUP * HEAD)
+        key_cols = pl.ds(pl.multiple_of(head * HEAD, HEAD), HEAD)
+        loads.append(pltpu.make_async_copy(og_hbm.at[:, query_cols], held.at[:, O_COLS], sem.at[i]))
+        for j, (source, cols, at) in enumerate(
+            [(q_hbm, query_cols, Q_COLS), (nk_hbm, key_cols, K_COLS), (nv_hbm, key_cols, V_COLS)]
+        ):
+            late.append(
+                pltpu.make_async_copy(source.at[:, cols], held.at[:, at], sem.at[2 + 3 * i + j])
+            )
+    for copy in loads + late:
+        copy.start()
+    shape = (own_ref.shape[0], HEAD)
+    tok = lax.broadcasted_iota(jnp.int32, shape, 0)
+    weight = jnp.zeros(shape, jnp.float32)
+    end = 0
+    for r in range(len_ref.shape[1]):
+        begin, end = end, end + len_ref[0, r]
+        weight = jnp.where((tok >= begin) & (tok < end), adv_ref[0, r], weight)
+    for copy, held in zip(loads, (send_ref, own_ref)):
+        copy.wait()
+        for g in range(GROUP):
+            cols = slice(HALF + g * HEAD, HALF + (g + 1) * HEAD)
+            held[:, cols] = (weight * held[:, cols].astype(jnp.float32)).astype(jnp.bfloat16)
+    for copy in late:
+        copy.wait()
 
 
 def pack(lengths, advantage, query, out_grad, near_key, near_value):
     smem = pl.BlockSpec(memory_space=pltpu.SMEM)
     vmem = pl.BlockSpec(memory_space=pltpu.VMEM)
     here = pl.BlockSpec(memory_space=pl.ANY)
+    shape = jax.ShapeDtypeStruct((query.shape[0], 2 * HALF), jnp.bfloat16)
     return pl.pallas_call(
         pack_kernel,
         in_specs=[smem, smem] + [here] * 4,
-        out_specs=[vmem, smem],
-        out_shape=[
-            jax.ShapeDtypeStruct((query.shape[0], 2 * HALF), jnp.bfloat16),
-            jax.ShapeDtypeStruct((1, 2 * lengths.shape[1]), jnp.float32),
-        ],
-        scratch_shapes=[pltpu.SemaphoreType.DMA((4,))],
+        out_specs=[vmem, vmem],
+        out_shape=[shape, shape],
+        scratch_shapes=[pltpu.SemaphoreType.DMA((8,))],
         name="pack",
     )(lengths, advantage, query, out_grad, near_key, near_value)
 
@@ -344,23 +345,25 @@
         name="rows",
     )(prompt_key, prompt_values)
     block = exchange(first, NEAR)
-    send, scalars = pack(lengths, advantage, query, out_grad, response_keys, response_values)
-    if TIE:
-        block, send, scalars = lax.optimization_barrier((block, send, scalars))
+    kept, send = pack(lengths, advantage, query, out_grad, response_keys, response_values)
+    block, kept, send, late_lengths = lax.optimization_barrier((block, kept, send, lengths))
     got = lax.ppermute(send, "zl", SWAP)
-    got_scalars = lax.ppermute(scalars, "zl", SWAP)
+    got_lengths = lax.ppermute(late_lengths, "zl", SWAP)
     kv = exchange(jnp.broadcast_to(block[None], (x * y, *block.shape)).reshape(-1, 2 * HEAD), FAR)
 
     def like(a, dtype=jnp.bfloat16):
         return jax.ShapeDtypeStruct(a.shape, dtype)
 
-    grad_query, grad_resp_key, grad_resp_value, sums = attention(
-        0, (lengths, advantage), (query, out_grad, response_keys, response_values, kv),
-        [like(query), like(response_keys), like(response_values), like(kv, jnp.float32)],
+    sums, = attention(0, True, False, (lengths,), (kept, kv), [like(kv, jnp.float32)])
+    back_shape = jax.ShapeDtypeStruct((query.shape[0], (GROUP + 2) * HEAD), jnp.bfloat16)
+    back, grad_kv = attention(
+        1, True, True, (got_lengths,), (got, kv, sums), [back_shape, like(kv)]
     )
-    back_shape = jax.ShapeDtypeStruct((query.shape[0], (GROUP + 2) * HEAD), jnp.bfloat16)
-    back, grad_kv = attention(1, (got_scalars,), (got, kv, sums), [back_shape, like(kv)])
-
+    kv, grad_kv = lax.optimization_barrier((kv, grad_kv))
+    grad_query, grad_resp_key, grad_resp_value = attention(
+        0, False, True, (lengths,), (kept, kv),
+        [like(query), like(response_keys), like(response_values)],
+    )
     back = lax.ppermute(back, "zl", SWAP)
     part = exchange(grad_kv, FAR).reshape(x * y, *block.shape)
     part = jnp.sum(part.astype(jnp.float32), axis=0).astype(jnp.bfloat16)

time: 105 us -> 104 us (level)
  waiting for transfers between devices: 47.4 us -> 37.7 us
  Pallas kernels: 25 us -> 30.9 us
  local copies, waits for them, and re-layouts: 1.83 us -> 3.13 us
  other arithmetic: 0.83 us -> 2.07 us
    all_to_all x4, waiting for transfers between devices: 47.4 us -> 37.7 us  [exchange(): return lax.all_to_all(a, axes, split_axis=0, concat_axis=0, tiled=True)]
    pallas_call x2 -> x3, Pallas kernels: 20.8 us -> 26.1 us  [attention(): pl.pallas_call(functools.partial(attention_kernel, part, prompt_side, tok...]
    reduce_sum x1, other arithmetic: 0.81 us -> 2.05 us  [on_device(): part = jnp.sum(part.astype(jnp.float32), axis=0).astype(jnp.bfloat16)]
  transfers between devices with their start and end apart: 7 -> 7, of which waited for: 4 -> 4; matrix products, arithmetic and copies ran while one was open for 1% -> 3% of each run, Pallas kernels for 13% -> 19%
where the time goes in v6:
time: 104 us; the launch traced here: 103 us
  waiting for transfers between devices  37.7 us (36%)
  Pallas kernels  30.9 us (30%)
  starting transfers between devices  28.7 us (28%)
  local copies, waits for them, and re-layouts  3.13 us (3%)
  other arithmetic  2.07 us (2%)
    all_to_all x4, waiting for transfers between devices, exchange(): return lax.all_to_all(a, axes, split_axis=0, concat_axis=0, tiled=True)  37.7 us
    all_to_all x4, starting transfers between devices, exchange(): return lax.all_to_all(a, axes, split_axis=0, concat_axis=0, tiled=True)  27.1 us
    pallas_call x3, Pallas kernels, attention(): pl.pallas_call(functools.partial(attention_kernel, part, prompt_side, tok...  26.1 us
    pallas_call x1, Pallas kernels, pack(): pl.pallas_call(pack_kernel, in_specs=[smem, smem] + [here] * 4, out_specs...  3.34 us
  transfers between devices with their start and end apart: 7, of which 4 were waited for; matrix products, arithmetic and copies ran while one was open for 3% of the time, Pallas kernels for 19%

profile of v6, /device:TPU:1, one launch (start us, length us, event | category | flops | bytes accessed | tf_op | source)
XLA Modules:
  0.0 103.2 jit_solution(7383491641332813133)
XLA Ops:
  0.6 1.4 %rows.1 = bf16[256,256]{1,0:T(8,128)(2,1)} custom-call(bf16[8,1024]{1,0:T(8,128)(2,1)} %key_ref.1, bf16[8,1024]{1,0:T(8,128)(2,1)} %value_ref.1), custom_call_target="tpu_custom_call" | custom-call | tf_op jit(solution)/shard_map/rows/pallas_call | solution.py:342
  2.0 12.8 %all-to-all-start = ((bf16[32,8,256]{2,1,0:T(8,128)(2,1)}), bf16[32,8,256]{2,1,0:T(8,128)(2,1)S(1)}, u32[]{:S(2)}, u32[]{:S(2)}) async-start(bf16[32,8,256]{2,1,0:T(8,128)(2,1)} %bitcast.13), calls=%async_computation | async-start | bytes 262144 | tf_op jit(solution)/shard_map/all_to_all | solution.py:253
  14.8 3.3 %pack.1 = (bf16[256,1536]{1,0:T(8,128)(2,1)}, bf16[256,1536]{1,0:T(8,128)(2,1)}) custom-call(s32[1,2]{1,0:T(1,128)} %refs_0_.3, f32[1,2]{1,0:T(1,128)} %adv_ref.1, bf16[256,1280]{1,0:T(8,128)(2,1)} %q_hbm.1, bf16[256,1280]{1,0:T(8,128)(2,1)} %og_hbm.1, bf16[256,256]{1,0:T(8,128)(2,1)} %nk_hbm.1, bf16[256,256]{1,0:T(8,128)(2,1)} %nv_hbm.1), custom_call_target="tpu_custom_call" | custom-call | tf_op jit(solution)/shard_map/pack/pallas_call | solution.py:311
  18.2 7.4 %all-to-all-done = bf16[32,8,256]{2,1,0:T(8,128)(2,1)S(1)} async-done(((bf16[32,8,256]{2,1,0:T(8,128)(2,1)}), bf16[32,8,256]{2,1,0:T(8,128)(2,1)S(1)}, u32[]{:S(2)}, u32[]{:S(2)}) %all-to-all-start) | async-done | bytes 131104 | tf_op jit(solution)/shard_map/all_to_all | solution.py:253
  25.6 1.1 %broadcast_in_dim.2 = bf16[8,256,256]{2,1,0:T(8,128)(2,1)} broadcast(bf16[256,256]{1,0:T(8,128)(2,1)S(1)} %bitcast.12), dimensions={1,2} | broadcast | bytes 1179648 | tf_op jit(solution)/shard_map/broadcast_in_dim | solution.py:352
  26.6 4.1 %all-to-all-start.1 = ((bf16[8,256,256]{2,1,0:T(8,128)(2,1)}), bf16[8,256,256]{2,1,0:T(8,128)(2,1)S(1)}, u32[]{:S(2)}, u32[]{:S(2)}) async-start(bf16[8,256,256]{2,1,0:T(8,128)(2,1)} %broadcast_in_dim.2), calls=%async_computation.1 | async-start | bytes 2097152 | tf_op jit(solution)/shard_map/all_to_all | solution.py:253
  30.7 0.4 collective-permute-start.1
  31.1 1.1 %collective-permute-start = (s32[1,2]{1,0:T(1,128)S(1)}, s32[1,2]{1,0:T(1,128)S(1)}, u32[]{:S(2)}, u32[]{:S(2)}) collective-permute-start(s32[1,2]{1,0:T(1,128)S(1)} %copy-done), channel_id=1, source_target_pairs={{0,4},{4,0},{1,5},{5,1},{2,6},{6,2},{3,7},{7,3},{8,12},{12,8},{9,1... | collective-permute-start | bytes 32 | tf_op jit(solution)/shard_map/ppermute | solution.py:351
  32.2 14.5 %all-to-all-done.1 = bf16[8,256,256]{2,1,0:T(8,128)(2,1)S(1)} async-done(((bf16[8,256,256]{2,1,0:T(8,128)(2,1)}), bf16[8,256,256]{2,1,0:T(8,128)(2,1)S(1)}, u32[]{:S(2)}, u32[]{:S(2)}) %all-to-all-start.1) | async-done | bytes 1048608 | tf_op jit(solution)/shard_map/all_to_all | solution.py:253
  46.7 7.9 %attention.3.refs_3_ = f32[2048,256]{1,0:T(8,128)S(1)} custom-call(s32[1,2]{1,0:T(1,128)S(1)} %copy-done, bf16[256,1536]{1,0:T(8,128)(2,1)S(1)} %copy-done.1, bf16[2048,256]{1,0:T(8,128)(2,1)S(1)} %bitcast.9), custom_call_target="tpu_custom_call" | custom-call | flops 4529848320 | bytes 4194304 | tf_op jit(solution)/shard_map/attention/pallas_call | solution.py:213
  54.7 10.0 %attention.4 = (bf16[256,896]{1,0:T(8,128)(2,1)S(1)}, bf16[2048,256]{1,0:T(8,128)(2,1)}) custom-call(s32[1,2]{1,0:T(1,128)S(1)} %collective-permute-done.refs_0_, bf16[256,1536]{1,0:T(8,128)(2,1)S(1)} %collective-permute-done.1.refs_1_, bf16[2048,256]{1,0:T(8,128)(2,1)S(1)} %bitcast.10, f32[2048,256]{1,0:T(8,128)S(1)} %attention.3.refs_3_), custom_call_target="tpu_custom_call" | custom-call | flops 4529848320 | bytes 4194304 | tf_op jit(solution)/shard_map/attention/pallas_call | solution.py:213
  64.7 4.2 %all-to-all-start.2 = ((bf16[8,256,256]{2,1,0:T(8,128)(2,1)}), bf16[8,256,256]{2,1,0:T(8,128)(2,1)}, u32[]{:S(2)}, u32[]{:S(2)}) async-start(bf16[8,256,256]{2,1,0:T(8,128)(2,1)} %bitcast.3), calls=%async_computation.2 | async-start | bytes 2097152 | tf_op jit(solution)/shard_map/all_to_all | solution.py:253
  69.0 0.1 collective-permute-start.2
  69.1 8.2 %attention.5 = (bf16[256,1280]{1,0:T(8,128)(2,1)}, bf16[256,256]{1,0:T(8,128)(2,1)}, bf16[256,256]{1,0:T(8,128)(2,1)}) custom-call(s32[1,2]{1,0:T(1,128)S(1)} %copy-done, bf16[256,1536]{1,0:T(8,128)(2,1)S(1)} %copy-done.1, bf16[2048,256]{1,0:T(8,128)(2,1)S(1)} %bitcast.11), custom_call_target="tpu_custom_call" | custom-call | flops 4529848320 | bytes 4194304 | tf_op jit(solution)/shard_map/attention/pallas_call | solution.py:213
  77.2 6.4 %all-to-all-done.2 = bf16[8,256,256]{2,1,0:T(8,128)(2,1)} async-done(((bf16[8,256,256]{2,1,0:T(8,128)(2,1)}), bf16[8,256,256]{2,1,0:T(8,128)(2,1)}, u32[]{:S(2)}, u32[]{:S(2)}) %all-to-all-start.2) | async-done | bytes 1048608 | tf_op jit(solution)/shard_map/all_to_all | solution.py:253
  83.7 2.1 %reduce_sum.21 = bf16[256,256]{1,0:T(8,128)(2,1)} reduce(bf16[8,256,256]{2,1,0:T(8,128)(2,1)} %all-to-all-done.2, bf16[]{:T(256)} %constant.21.clone.1), dimensions={0}, to_apply=%region_0.0 | reduce | flops 458752 | bytes 1179650 | tf_op jit(solution)/shard_map/reduce_sum | solution.py:369
  85.7 6.0 %all-to-all-start.3 = ((bf16[32,8,256]{2,1,0:T(8,128)(2,1)}), bf16[32,8,256]{2,1,0:T(8,128)(2,1)S(1)}, u32[]{:S(2)}, u32[]{:S(2)}) async-start(bf16[32,8,256]{2,1,0:T(8,128)(2,1)} %bitcast.4), calls=%async_computation.3 | async-start | bytes 262144 | tf_op jit(solution)/shard_map/all_to_all | solution.py:253
  91.7 0.7 slice_dynamic-update-slice_fusion.1
  92.4 0.8 slice_dynamic-update-slice_fusion
  93.2 9.3 %all-to-all-done.3 = bf16[32,8,256]{2,1,0:T(8,128)(2,1)S(1)} async-done(((bf16[32,8,256]{2,1,0:T(8,128)(2,1)}), bf16[32,8,256]{2,1,0:T(8,128)(2,1)S(1)}, u32[]{:S(2)}, u32[]{:S(2)}) %all-to-all-start.3) | async-done | bytes 131104 | tf_op jit(solution)/shard_map/all_to_all | solution.py:253
  102.6 0.0 copy-start.2
  102.6 0.0 copy-start.3
  102.6 0.6 copy-done.2
  103.2 0.0 copy-done.3
  (16 shorter events, 0.1 us)
Async XLA Ops:
  2.0 23.5 %all-to-all-start = ((bf16[32,8,256]{2,1,0:T(8,128)(2,1)}), bf16[32,8,256]{2,1,0:T(8,128)(2,1)S(1)}, u32[]{:S(2)}, u32[]{:S(2)}) async-start(bf16[32,8,256]{2,1,0:T(8,128)(2,1)} %bitcast.13), calls=%async_computation | async-start | bytes 262144 | tf_op jit(solution)/shard_map/all_to_all | solution.py:253
  14.8 16.3 %copy-start = (s32[1,2]{1,0:T(1,128)S(1)}, s32[1,2]{1,0:T(1,128)}, u32[]{:S(2)}) copy-start(s32[1,2]{1,0:T(1,128)} %refs_0_.3) | copy-start | bytes 28
  18.1 28.6 %copy-start.1 = (bf16[256,1536]{1,0:T(8,128)(2,1)S(1)}, bf16[256,1536]{1,0:T(8,128)(2,1)}, u32[]{:S(2)}) copy-start(bf16[256,1536]{1,0:T(8,128)(2,1)} %get-tuple-element.20.refs_1_) | copy-start | bytes 2359300
  26.6 20.1 %all-to-all-start.1 = ((bf16[8,256,256]{2,1,0:T(8,128)(2,1)}), bf16[8,256,256]{2,1,0:T(8,128)(2,1)S(1)}, u32[]{:S(2)}, u32[]{:S(2)}) async-start(bf16[8,256,256]{2,1,0:T(8,128)(2,1)} %broadcast_in_dim.2), calls=%async_computation.1 | async-start | bytes 2097152 | tf_op jit(solution)/shard_map/all_to_all | solution.py:253
  30.7 23.9 %collective-permute-start.1 = (bf16[256,1536]{1,0:T(8,128)(2,1)}, bf16[256,1536]{1,0:T(8,128)(2,1)S(1)}, u32[]{:S(2)}, u32[]{:S(2)}) collective-permute-start(bf16[256,1536]{1,0:T(8,128)(2,1)} %get-tuple-element.23), channel_id=1, source_target_pairs={{0,4},{4,0},{1,5},{5,1},{2,6},{6,2},{3,7},{7,3},{8,12},{12,8},{9,1... | collective-permute-start | bytes 2359304 | tf_op jit(solution)/shard_map/ppermute | solution.py:350
  31.1 23.5 %collective-permute-start = (s32[1,2]{1,0:T(1,128)S(1)}, s32[1,2]{1,0:T(1,128)S(1)}, u32[]{:S(2)}, u32[]{:S(2)}) collective-permute-start(s32[1,2]{1,0:T(1,128)S(1)} %copy-done), channel_id=1, source_target_pairs={{0,4},{4,0},{1,5},{5,1},{2,6},{6,2},{3,7},{7,3},{8,12},{12,8},{9,1... | collective-permute-start | bytes 32 | tf_op jit(solution)/shard_map/ppermute | solution.py:351
  64.7 19.0 %all-to-all-start.2 = ((bf16[8,256,256]{2,1,0:T(8,128)(2,1)}), bf16[8,256,256]{2,1,0:T(8,128)(2,1)}, u32[]{:S(2)}, u32[]{:S(2)}) async-start(bf16[8,256,256]{2,1,0:T(8,128)(2,1)} %bitcast.3), calls=%async_computation.2 | async-start | bytes 2097152 | tf_op jit(solution)/shard_map/all_to_all | solution.py:253
  69.0 22.8 %collective-permute-start.2 = (bf16[256,896]{1,0:T(8,128)(2,1)S(1)}, bf16[256,896]{1,0:T(8,128)(2,1)S(1)}, u32[]{:S(2)}, u32[]{:S(2)}) collective-permute-start(bf16[256,896]{1,0:T(8,128)(2,1)S(1)} %get-tuple-element.27), channel_id=1, source_target_pairs={{0,4},{4,0},{1,5},{5,1},{2,6},{6,2},{3,7},{7,3},{8,12},{12,8},{9,1... | collective-permute-start | bytes 1376264 | tf_op jit(solution)/shard_map/ppermute | solution.py:367
  85.7 16.8 %all-to-all-start.3 = ((bf16[32,8,256]{2,1,0:T(8,128)(2,1)}), bf16[32,8,256]{2,1,0:T(8,128)(2,1)S(1)}, u32[]{:S(2)}, u32[]{:S(2)}) async-start(bf16[32,8,256]{2,1,0:T(8,128)(2,1)} %bitcast.4), calls=%async_computation.3 | async-start | bytes 262144 | tf_op jit(solution)/shard_map/all_to_all | solution.py:253
  102.6 0.6 copy-start.2
  102.6 0.6 copy-start.3
